TPU v7x, 32 devices: a whole 2x2x4 slice. The times are simulated.
32 devices in a mesh: groups: 2 (over y), shot: 4 (over z), sub: 2 (over x), rep: 2 (over core).
Axes of the slice: x: 2, y: 2, z: 4, core: 2. Of those that a mesh axis runs over, the one named last changes fastest.
Arguments:
- model: float32 [256, 3, 640], P(('groups', 'shot')), parts along dimension 0, may hold values from 1 to 2.5
- accum: float32 [256, 3, 640], P(('groups', 'shot')), parts along dimension 0, may hold values from 1 to 100
- owner_map: int32 [256], P('groups'), parts along dimension 0, may hold values from 0 to 127, as said below
- aperture: int32 [8, 2, 32], P('groups', 'sub'), parts along dimension 0, may hold values from 0 to 127, as said below
- start_state: bfloat16 [8, 2, 1, 9, 16, 80, 32], P(('groups', 'shot'), 'rep', None, None, 'sub'), parts along dimension 0, may hold values from -6 to 6
- adjoint_end: bfloat16 [8, 2, 1, 9, 16, 80, 32], P(('groups', 'shot'), 'rep', None, None, 'sub'), parts along dimension 0, may hold values from -6 to 6
- wavelet: float32 [8, 2, 1, 2], P(('groups', 'shot'), 'rep'), parts along dimension 0, may hold values from -24 to 24
- source_cell: int32 [8, 2, 1], P(('groups', 'shot'), 'rep'), parts along dimension 0, may hold values from 0 to 40959
- receiver_cell: int32 [8, 2, 1, 256], P(('groups', 'shot'), 'rep'), parts along dimension 0, may hold values from 0 to 40959
- observed: float32 [8, 2, 1, 2, 256], P(('groups', 'shot'), 'rep'), parts along dimension 0, may hold values from -6 to 6
Outputs:
- new_model: float32 [256, 3, 640], P(('groups', 'shot')), parts along dimension 0
- new_accum: float32 [256, 3, 640], P(('groups', 'shot')), parts along dimension 0
There are 2 independent parts, one for each index of `groups`. A program takes and returns all parts, laid end to end along the dimension named above; each array names one. Nothing has to cross between parts.
Inputs may be any that keep to these rules, and one draw needn't show every extreme that they name: `owner_map`: A permutation: each tile's storage slot; the owner of a tile is its slot // 32. The 32 ids of one slab aperture[s, u, :] are distinct; at most 16 of them have one owner, and in every slab some owner has exactly 16. All replicas of shot s share its aperture.
All inputs are finite; a program needn't handle non-finite values.
Results may differ from a plain program's by a relative error of at most 0.0003.
Values sent between devices are 32-bit elements; how exact they have to be, the bound alone decides.
A program may use at most 64 MiB of HBM per device.

v0:
```python
import jax
import jax.numpy as jnp
from jax import lax
from jax.sharding import PartitionSpec as P

DEPTH = 32
TILE_X = 4
TILE_Y = 5
SLAB_XT = 2
SLAB_YT = 16
NSTEPS = 2
SLAB_TILES = 32


time_step = 0.18
learn_rate = 0.5


def passed_along(block, axis, distance):
    devices = range(lax.axis_size(axis))
    route = [(i - distance, i) for i in devices if i - distance in devices]
    return lax.ppermute(block, axis, route)


def plus_x(field, right):
    return jnp.concatenate([field[:, 1:], right], axis=1) - field


def minus_x(field, left):
    return field - jnp.concatenate([left, field[:, :-1]], axis=1)


def plus_y(field):
    return jnp.concatenate([field[:, :, 1:], jnp.zeros_like(field[:, :, :1])], axis=2) - field


def minus_y(field):
    return field - jnp.concatenate([jnp.zeros_like(field[:, :, :1]), field[:, :, :-1]], axis=2)


def plus_z(field):
    return jnp.concatenate([field[:, :, :, 1:], jnp.zeros_like(field[:, :, :, :1])], axis=3) - field


def minus_z(field):
    return field - jnp.concatenate(
        [jnp.zeros_like(field[:, :, :, :1]), field[:, :, :, :-1]], axis=3
    )


def velocity_half(state, density, left_rim, right_rim):
    buoyancy = 1.0 / density
    vel_x, vel_y, vel_z = (state[:, 0], state[:, 1], state[:, 2])
    stress_xx, stress_yy, stress_zz = (state[:, 3], state[:, 4], state[:, 5])
    stress_xy, stress_xz, stress_yz = (state[:, 6], state[:, 7], state[:, 8])
    new_x = vel_x + time_step * buoyancy * (
        plus_x(stress_xx, right_rim[:, 0]) + minus_y(stress_xy) + minus_z(stress_xz)
    )
    new_y = vel_y + time_step * buoyancy * (
        minus_x(stress_xy, left_rim[:, 0]) + plus_y(stress_yy) + minus_z(stress_yz)
    )
    new_z = vel_z + time_step * buoyancy * (
        minus_x(stress_xz, left_rim[:, 1]) + minus_y(stress_yz) + plus_z(stress_zz)
    )
    return jnp.concatenate([jnp.stack([new_x, new_y, new_z], axis=1), state[:, 3:]], axis=1)


def stress_half(state, lame, shear, left_rim, right_rim):
    vel_x, vel_y, vel_z = (state[:, 0], state[:, 1], state[:, 2])
    strain_xx = minus_x(vel_x, left_rim[:, 0])
    strain_yy = minus_y(vel_y)
    strain_zz = minus_z(vel_z)
    volume = strain_xx + strain_yy + strain_zz
    new_xx = state[:, 3] + time_step * (lame * volume + 2.0 * shear * strain_xx)
    new_yy = state[:, 4] + time_step * (lame * volume + 2.0 * shear * strain_yy)
    new_zz = state[:, 5] + time_step * (lame * volume + 2.0 * shear * strain_zz)
    new_xy = state[:, 6] + time_step * shear * (plus_y(vel_x) + plus_x(vel_y, right_rim[:, 0]))
    new_xz = state[:, 7] + time_step * shear * (plus_z(vel_x) + plus_x(vel_z, right_rim[:, 1]))
    new_yz = state[:, 8] + time_step * shear * (plus_z(vel_y) + plus_y(vel_z))
    stresses = jnp.stack([new_xx, new_yy, new_zz, new_xy, new_xz, new_yz], axis=1)
    return jnp.concatenate([state[:, :3], stresses], axis=1)


def trade(first, last):
    from_prior = passed_along(last, "sub", 1)
    from_next = passed_along(first, "sub", -1)
    return (from_prior, from_next)


def on_device(
    model,
    accum,
    owner_map,
    aperture,
    start_state,
    adjoint_end,
    wavelet,
    source_cell,
    receiver_cell,
    observed,
):
    n_shot = lax.axis_size("shot")
    my_shot = lax.axis_index("shot")
    my_sub = lax.axis_index("sub")
    tiles_dev = model.shape[0]
    tile_cells = model.shape[2]
    per_owner = 2 * SLAB_TILES // n_shot
    slab_slots = owner_map[aperture[:, 0, :]]
    owners = slab_slots // tiles_dev
    local_rows = slab_slots % tiles_dev
    positions = jnp.arange(SLAB_TILES, dtype=jnp.int32)
    earlier = (owners[:, :, None] == owners[:, None, :]) & (
        positions[None, None, :] < positions[None, :, None]
    )
    ranks = jnp.sum(earlier.astype(jnp.int32), axis=2)
    slot_ids = jnp.arange(per_owner, dtype=jnp.int32)
    serve = (owners[:, None, :] == my_shot) & (ranks[:, None, :] == slot_ids[None, :, None])
    served = jnp.any(serve, axis=2)
    serve_rows = jnp.sum(jnp.where(serve, local_rows[:, None, :], 0), axis=2)
    outgoing = jnp.where(served[:, :, None, None], model[serve_rows], 0.0)
    incoming = lax.all_to_all(outgoing, "shot", split_axis=0, concat_axis=0, tiled=True)
    my_owners = owners[my_shot]
    my_ranks = ranks[my_shot]
    slab = incoming.reshape(n_shot * per_owner, 3, tile_cells)[my_owners * per_owner + my_ranks]
    slab_x = SLAB_XT * TILE_X
    slab_y = SLAB_YT * TILE_Y
    params = slab.reshape(SLAB_XT, SLAB_YT, 3, TILE_X, TILE_Y, DEPTH)
    params = params.transpose(2, 0, 3, 1, 4, 5).reshape(3, slab_x, slab_y, DEPTH)
    lame, shear, density = (params[0], params[1], params[2])
    state = start_state[0, 0].astype(jnp.float32)
    shots = state.shape[0]
    cells = slab_x * slab_y * DEPTH
    offset = my_sub * cells
    source_local = source_cell[0, 0] - offset
    onehot = (jnp.arange(cells, dtype=jnp.int32)[None, :] == source_local[:, None]).astype(
        jnp.float32
    )
    onehot = onehot.reshape(shots, slab_x, slab_y, DEPTH)
    receiver_local = receiver_cell[0, 0] - offset
    receiver_live = (receiver_local >= 0) & (receiver_local < cells)
    receiver_rows = jnp.clip(receiver_local, 0, cells - 1)
    shot_rows = jnp.arange(shots, dtype=jnp.int32)[:, None]
    amplitudes = wavelet[0, 0]
    recorded_obs = observed[0, 0]
    saved = []
    residuals = []
    for number in range(NSTEPS):
        left_rim, right_rim = trade(state[:, 3:4, 0:1], state[:, 6:8, -1:])
        saved.append((state, left_rim, right_rim))
        state = velocity_half(state, density, left_rim, right_rim)
        left_rim, right_rim = trade(state[:, 1:3, 0:1], state[:, 0:1, -1:])
        saved.append((state, left_rim, right_rim))
        state = stress_half(state, lame, shear, left_rim, right_rim)
        source = time_step * amplitudes[:, number][:, None, None, None] * onehot
        state = state.at[:, 3:6].add(source[:, None])
        recorded = jnp.take_along_axis(state[:, 2].reshape(shots, cells), receiver_rows, axis=1)
        residuals.append(jnp.where(receiver_live, recorded - recorded_obs[:, number], 0.0))
    cotangent = adjoint_end[0, 0].astype(jnp.float32)
    grad_lame = jnp.zeros_like(lame)
    grad_shear = jnp.zeros_like(shear)
    grad_density = jnp.zeros_like(density)
    for number in reversed(range(NSTEPS)):
        flat_vz = (
            cotangent[:, 2]
            .reshape(shots, cells)
            .at[shot_rows, receiver_rows]
            .add(residuals[number])
        )
        cotangent = cotangent.at[:, 2].set(flat_vz.reshape(shots, slab_x, slab_y, DEPTH))
        state_in, left_rim, right_rim = saved[2 * number + 1]
        _, backward = jax.vjp(stress_half, state_in, lame, shear, left_rim, right_rim)
        cotangent, part_lame, part_shear, cot_left, cot_right = backward(cotangent)
        grad_lame = grad_lame + part_lame
        grad_shear = grad_shear + part_shear
        add_first, add_last = trade(cot_left, cot_right)
        cotangent = cotangent.at[:, 0:1, -1:].add(add_last)
        cotangent = cotangent.at[:, 1:3, 0:1].add(add_first)
        state_in, left_rim, right_rim = saved[2 * number]
        _, backward = jax.vjp(velocity_half, state_in, density, left_rim, right_rim)
        cotangent, part_density, cot_left, cot_right = backward(cotangent)
        grad_density = grad_density + part_density
        add_first, add_last = trade(cot_left, cot_right)
        cotangent = cotangent.at[:, 6:8, -1:].add(add_last)
        cotangent = cotangent.at[:, 3:4, 0:1].add(add_first)
    gradient = jnp.stack([grad_lame, grad_shear, grad_density], axis=0)
    back = gradient.reshape(3, SLAB_XT, TILE_X, SLAB_YT, TILE_Y, DEPTH)
    back = back.transpose(1, 3, 0, 2, 4, 5).reshape(SLAB_TILES, 3, tile_cells)
    all_slots = jnp.arange(per_owner, dtype=jnp.int32)
    owner_ids = jnp.arange(n_shot, dtype=jnp.int32)
    place = (my_owners[None, None, :] == owner_ids[:, None, None]) & (
        my_ranks[None, None, :] == all_slots[None, :, None]
    )
    placed = jnp.any(place, axis=2)
    place_rows = jnp.sum(jnp.where(place, positions[None, None, :], 0), axis=2)
    returning = jnp.where(placed[:, :, None, None], back[place_rows], 0.0)
    arrived = lax.all_to_all(returning, "shot", split_axis=0, concat_axis=0, tiled=True)
    pick = (
        serve_rows[:, :, None] == jnp.arange(tiles_dev, dtype=jnp.int32)[None, None, :]
    ) & served[:, :, None]
    pick = pick.astype(jnp.float32).reshape(n_shot * per_owner, tiles_dev)
    partial_sum = jnp.einsum(
        "sd,sc->dc",
        pick,
        arrived.reshape(n_shot * per_owner, 3 * tile_cells),
        precision=lax.Precision.HIGHEST,
        preferred_element_type=jnp.float32,
    )
    partial_sum = partial_sum.reshape(tiles_dev, 3, tile_cells)
    total = lax.psum(partial_sum, ("sub", "rep"))
    new_accum = accum + total * total
    new_model = model - learn_rate * total / jnp.sqrt(new_accum)
    return (new_model, new_accum)


def solution(mesh):
    in_specs = (
        P(("groups", "shot"), None, None),
        P(("groups", "shot"), None, None),
        P("groups"),
        P("groups", "sub", None),
        P(("groups", "shot"), "rep", None, None, "sub", None, None),
        P(("groups", "shot"), "rep", None, None, "sub", None, None),
        P(("groups", "shot"), "rep", None, None),
        P(("groups", "shot"), "rep", None),
        P(("groups", "shot"), "rep", None, None),
        P(("groups", "shot"), "rep", None, None, None),
    )
    out_specs = (P(("groups", "shot"), None, None), P(("groups", "shot"), None, None))
    return jax.shard_map(
        on_device, mesh=mesh, in_specs=in_specs, out_specs=out_specs, check_vma=False
    )
```

profile of v0, /device:TPU:1, one launch (start us, length us, event | category | flops | bytes accessed | tf_op | source)
XLA Modules:
  0.0 212.7 jit_solution(12678889331934372388)
XLA Ops:
  8.1 1.2 gather_fusion
  10.2 1.3 gather_fusion.1
  12.5 5.4 %all-to-all-start = ((f32[4,16,3,640]{3,1,2,0:T(8,128)}), f32[4,16,3,640]{3,1,2,0:T(8,128)S(1)}, u32[]{:S(2)}, u32[]{:S(2)}) async-start(f32[4,16,3,640]{3,1,2,0:T(8,128)} %copy_select_fusion.1), calls=%async_computation | async-start | bytes 983040 | tf_op jit(solution)/shard_map/all_to_all | solution.py:121
  18.7 3.1 %collective-permute-start = (f32[1,2,1,80,32]{3,4,2,1,0:T(8,128)}, f32[1,2,1,80,32]{3,4,2,1,0:T(8,128)S(1)}, u32[]{:S(2)}, u32[]{:S(2)}) collective-permute-start(f32[1,2,1,80,32]{3,4,2,1,0:T(8,128)} %slice.799), channel_id=1, source_target_pairs={{0,2},{1,3},{4,6},{5,7},{8,10},{9,11},{12,14},{13,15},{16,18},{17,... | collective-permute-start | bytes 61448 | tf_op jit(solution)/shard_map/ppermute | solution.py:22
  22.4 1.3 collective-permute-start.1
  28.0 1.2 bitcast_convert_fusion.1
  35.6 1.8 gather_fusion.2
  37.4 1.7 reshape.2102
  39.1 2.0 copy.352
  43.0 1.1 copy.284
  44.1 1.8 fusion.14
  46.0 2.1 fusion.12
  48.7 1.3 collective-permute-start.2
  57.7 5.1 %collective-permute-start.4 = (f32[1,1,1,80,32]{3,4,2,1,0:T(8,128)S(1)}, f32[1,1,1,80,32]{3,4,2,1,0:T(8,128)S(1)}, u32[]{:S(2)}, u32[]{:S(2)}) collective-permute-start(f32[1,1,1,80,32]{3,4,2,1,0:T(8,128)S(1)} %slice.832), channel_id=1, source_target_pairs={{0,2},{1,3},{4,6},{5,7},{8,10},{9,11},{12,14},{13,15},{16,18},{17,... | collective-permute-start | bytes 30728 | tf_op jit(solution)/shard_map/ppermute | solution.py:22
  63.7 1.1 copy.294
  64.8 1.8 copy.285
  67.8 1.9 copy.291
  69.6 1.8 copy.292
  72.5 1.8 copy.317
  74.3 1.8 copy.318
  76.1 1.7 gather_fusion.5
  79.2 2.2 %multiply_add_fusion.6 = (f32[1,8,80,32]{2,3,1,0:T(8,128)S(1)}, f32[1,8,80,32]{2,3,1,0:T(8,128)}, f32[1,1,8,80,32]{3,4,2,1,0:T(8,128)S(1)}, f32[1,8,80,32]{2,3,1...) fusion(f32[1,8,80,32]{2,3,1,0:T(8,128)S(1)} %copy.288, ...), kind=kLoop, calls=%fused_computation.176 | loop fusion | flops 450560 | bytes 2039808 | tf_op jit(solution)/shard_map/add | solution.py:77
  81.5 1.9 multiply_add_fusion.7
  83.4 1.3 collective-permute-start.3
  87.0 1.3 collective-permute-start.5
  89.4 1.7 gather_fusion.4
  91.8 2.0 scatter_fusion
  96.3 4.0 %collective-permute-start.8 = (f32[1,2,1,80,32]{3,4,2,1,0:T(8,128)S(1)}, f32[1,2,1,80,32]{3,4,2,1,0:T(8,128)S(1)}, u32[]{:S(2)}, u32[]{:S(2)}) collective-permute-start(f32[1,2,1,80,32]{3,4,2,1,0:T(8,128)S(1)} %pad_add_fusion.4), channel_id=1, source_target_pairs={{0,2},{1,3},{4,6},{5,7},{8,10},{9,11},{12,14},{13,15},{16,18},{17,... | collective-permute-start | bytes 61448 | tf_op jit(solution)/shard_map/ppermute | solution.py:22
  100.4 1.5 collective-permute-start.7
  102.5 2.4 %collective-permute-done.7 = f32[1,1,1,80,32]{3,4,2,1,0:T(8,128)S(1)} collective-permute-done((f32[1,1,1,80,32]{3,4,2,1,0:T(8,128)S(1)}, f32[1,1,1,80,32]{3,4,2,1,0:T(8,128)S(1)}, u32[]{:S(2)}, u32[]{:S(2)}) %collective-permute-start.7) | collective-permute-done | bytes 10272 | tf_op jit(solution)/shard_map/ppermute | solution.py:22
  104.9 1.9 fusion.72
  111.8 1.3 collective-permute-start.11
  113.1 1.3 collective-permute-start.9
  114.4 4.0 %collective-permute-start.10 = (f32[1,1,1,80,32]{3,4,2,1,0:T(8,128)S(1)}, f32[1,1,1,80,32]{3,4,2,1,0:T(8,128)S(1)}, u32[]{:S(2)}, u32[]{:S(2)}) collective-permute-start(f32[1,1,1,80,32]{3,4,2,1,0:T(8,128)S(1)} %slice_bitcast_fusion.21), channel_id=1, source_target_pairs={{0,2},{1,3},{4,6},{5,7},{8,10},{9,11},{12,14},{13,15},{16,18},{17,... | collective-permute-start | bytes 30728 | tf_op jit(solution)/shard_map/ppermute | solution.py:22
  118.4 1.3 collective-permute-start.6
  122.4 2.0 scatter_fusion.1
  125.2 1.1 copy.314
  132.3 1.2 fusion.37
  133.5 1.8 copy.316
  135.9 3.1 %collective-permute-start.13 = (f32[1,2,1,80,32]{3,4,2,1,0:T(8,128)}, f32[1,2,1,80,32]{3,4,2,1,0:T(8,128)}, u32[]{:S(2)}, u32[]{:S(2)}) collective-permute-start(f32[1,2,1,80,32]{3,4,2,1,0:T(8,128)} %pad_add_fusion.2), channel_id=1, source_target_pairs={{0,2},{1,3},{4,6},{5,7},{8,10},{9,11},{12,14},{13,15},{16,18},{17,... | collective-permute-start | bytes 61448 | tf_op jit(solution)/shard_map/ppermute | solution.py:22
  141.0 1.4 collective-permute-start.12
  142.5 1.4 add_bitcast_fusion.2
  145.8 1.9 fusion.73
  148.6 1.4 fusion.8
  153.2 4.5 %all-to-all-start.1 = ((f32[4,16,3,640]{3,1,2,0:T(8,128)}), f32[4,16,3,640]{3,1,2,0:T(8,128)S(1)}, u32[]{:S(2)}, u32[]{:S(2)}) async-start(f32[4,16,3,640]{3,1,2,0:T(8,128)} %copy_select_fusion), calls=%async_computation.1 | async-start | bytes 983040 | tf_op jit(solution)/shard_map/all_to_all | solution.py:196
  157.8 8.7 %all-to-all-done.1 = f32[4,16,3,640]{3,1,2,0:T(8,128)S(1)} async-done(((f32[4,16,3,640]{3,1,2,0:T(8,128)}), f32[4,16,3,640]{3,1,2,0:T(8,128)S(1)}, u32[]{:S(2)}, u32[]{:S(2)}) %all-to-all-start.1) | async-done | bytes 491552 | tf_op jit(solution)/shard_map/all_to_all | solution.py:196
  167.8 36.3 %all-reduce.87.cloned.1.call-done = f32[32,3,640]{2,0,1:T(8,128)} async-done(((f32[32,3,640]{2,0,1:T(8,128)}), f32[32,3,640]{2,0,1:T(8,128)}) %all-reduce.87.cloned.1.call-update) | async-done | bytes 245776 | tf_op jit(solution)/shard_map/psum | solution.py:209
  204.1 1.8 multiply_subtract_fusion
  (330 shorter events, 59.1 us)
Async XLA Ops:
  11.6 6.3 %copy-start.33 = (bf16[1,1,1,9,8,80,32]{5,6,4,3,2,1,0:T(8,128)(2,1)S(1)}, bf16[1,1,1,9,8,80,32]{5,6,4,3,2,1,0:T(8,128)(2,1)}, u32[]{:S(2)}) copy-start(bf16[1,1,1,9,8,80,32]{5,6,4,3,2,1,0:T(8,128)(2,1)} %param.36) | copy-start | bytes 1105924
  12.5 22.0 %all-to-all-start = ((f32[4,16,3,640]{3,1,2,0:T(8,128)}), f32[4,16,3,640]{3,1,2,0:T(8,128)S(1)}, u32[]{:S(2)}, u32[]{:S(2)}) async-start(f32[4,16,3,640]{3,1,2,0:T(8,128)} %copy_select_fusion.1), calls=%async_computation | async-start | bytes 983040 | tf_op jit(solution)/shard_map/all_to_all | solution.py:121
  18.1 6.5 %copy-start.67 = (s32[1,1,1,256]{3,2,1,0:T(1,128)S(1)}, s32[1,1,1,256]{3,2,1,0:T(1,128)}, u32[]{:S(2)}) copy-start(s32[1,1,1,256]{3,2,1,0:T(1,128)} %param.40) | copy-start | bytes 3076
  18.1 7.9 %copy-start.79 = (s32[5]{0:T(128)S(1)}, s32[5]{0:T(128)}, u32[]{:S(2)}) copy-start(s32[5]{0:T(128)} %constant.350.clone.1) | copy-start | bytes 64
  18.1 9.2 %copy-start.80 = (f32[1,1,1,2]{3,2,1,0:T(1,128)S(1)}, f32[1,1,1,2]{3,2,1,0:T(1,128)}, u32[]{:S(2)}) copy-start(f32[1,1,1,2]{3,2,1,0:T(1,128)} %param.38) | copy-start | bytes 28
  18.7 15.1 %collective-permute-start = (f32[1,2,1,80,32]{3,4,2,1,0:T(8,128)}, f32[1,2,1,80,32]{3,4,2,1,0:T(8,128)S(1)}, u32[]{:S(2)}, u32[]{:S(2)}) collective-permute-start(f32[1,2,1,80,32]{3,4,2,1,0:T(8,128)} %slice.799), channel_id=1, source_target_pairs={{0,2},{1,3},{4,6},{5,7},{8,10},{9,11},{12,14},{13,15},{16,18},{17,... | collective-permute-start | bytes 61448 | tf_op jit(solution)/shard_map/ppermute | solution.py:22
  22.4 23.5 %collective-permute-start.1 = (f32[1,1,1,80,32]{3,4,2,1,0:T(8,128)}, f32[1,1,1,80,32]{3,4,2,1,0:T(8,128)}, u32[]{:S(2)}, u32[]{:S(2)}) collective-permute-start(f32[1,1,1,80,32]{3,4,2,1,0:T(8,128)} %slice.810), channel_id=1, source_target_pairs={{2,0},{3,1},{6,4},{7,5},{10,8},{11,9},{14,12},{15,13},{18,16},{19,... | collective-permute-start | bytes 30728 | tf_op jit(solution)/shard_map/ppermute | solution.py:22
  24.5 6.8 %copy-start.30 = (f32[1,8,80,32]{2,3,1,0:T(8,128)}, f32[1,8,80,32]{2,3,1,0:T(8,128)S(1)}, u32[]{:S(2)}) copy-start(f32[1,8,80,32]{2,3,1,0:T(8,128)S(1)} %get-tuple-element.209) | copy-start | bytes 245764
  24.5 7.4 %copy-start.31 = (f32[1,8,80,32]{2,3,1,0:T(8,128)}, f32[1,8,80,32]{2,3,1,0:T(8,128)S(1)}, u32[]{:S(2)}) copy-start(f32[1,8,80,32]{2,3,1,0:T(8,128)S(1)} %get-tuple-element.213) | copy-start | bytes 245764
  24.5 19.6 %copy-start.29 = (f32[1,8,80,32]{2,3,1,0:T(8,128)}, f32[1,8,80,32]{2,3,1,0:T(8,128)S(1)}, u32[]{:S(2)}) copy-start(f32[1,8,80,32]{2,3,1,0:T(8,128)S(1)} %get-tuple-element.212) | copy-start | bytes 245764
  24.5 6.0 %copy-start.50 = (f32[1,8,80,32]{2,3,1,0:T(8,128)S(1)}, f32[1,8,80,32]{2,3,1,0:T(8,128)}, u32[]{:S(2)}) copy-start(f32[1,8,80,32]{2,3,1,0:T(8,128)} %get-tuple-element.208) | copy-start | bytes 245764
  27.3 4.0 %copy-start.57 = (f32[1,8,80,32]{2,3,1,0:T(8,128)S(1)}, f32[1,8,80,32]{2,3,1,0:T(8,128)}, u32[]{:S(2)}) copy-start(f32[1,8,80,32]{2,3,1,0:T(8,128)} %get-tuple-element.210) | copy-start | bytes 245764
  28.0 4.6 %copy-start.49 = (f32[1,8,80,32]{2,3,1,0:T(8,128)S(1)}, f32[1,8,80,32]{2,3,1,0:T(8,128)}, u32[]{:S(2)}) copy-start(f32[1,8,80,32]{2,3,1,0:T(8,128)} %get-tuple-element.211) | copy-start | bytes 245764
  46.0 4.0 %copy-start.74 = (s32[64]{0:T(128)S(1)}, s32[64]{0:T(128)}, u32[]{:S(2)}) copy-start(s32[64]{0:T(128)} %reshape.2052) | copy-start | bytes 772
  48.7 29.2 %collective-permute-start.2 = (f32[1,2,1,80,32]{3,4,2,1,0:T(8,128)}, f32[1,2,1,80,32]{3,4,2,1,0:T(8,128)}, u32[]{:S(2)}, u32[]{:S(2)}) collective-permute-start(f32[1,2,1,80,32]{3,4,2,1,0:T(8,128)} %pad_maximum_fusion.2), channel_id=1, source_target_pairs={{2,0},{3,1},{6,4},{7,5},{10,8},{11,9},{14,12},{15,13},{18,16},{19,... | collective-permute-start | bytes 61448 | tf_op jit(solution)/shard_map/ppermute | solution.py:22
  57.7 20.9 %collective-permute-start.4 = (f32[1,1,1,80,32]{3,4,2,1,0:T(8,128)S(1)}, f32[1,1,1,80,32]{3,4,2,1,0:T(8,128)S(1)}, u32[]{:S(2)}, u32[]{:S(2)}) collective-permute-start(f32[1,1,1,80,32]{3,4,2,1,0:T(8,128)S(1)} %slice.832), channel_id=1, source_target_pairs={{0,2},{1,3},{4,6},{5,7},{8,10},{9,11},{12,14},{13,15},{16,18},{17,... | collective-permute-start | bytes 30728 | tf_op jit(solution)/shard_map/ppermute | solution.py:22
  67.7 13.7 %copy-start.9 = (f32[1,8,80,32]{2,3,1,0:T(8,128)}, f32[1,8,80,32]{2,3,1,0:T(8,128)S(1)}, u32[]{:S(2)}) copy-start(f32[1,8,80,32]{2,3,1,0:T(8,128)S(1)} %copy.288) | copy-start | bytes 245764
  67.7 8.4 %copy-start.69 = (s32[1024]{0:T(1024)S(1)}, s32[1024]{0:T(1024)}, u32[]{:S(2)}) copy-start(s32[1024]{0:T(1024)} %pad_clamp_fusion.1) | copy-start | bytes 12292
  81.5 6.8 %copy-start.5 = (f32[1,8,80,32]{2,3,1,0:T(8,128)}, f32[1,8,80,32]{2,3,1,0:T(8,128)S(1)}, u32[]{:S(2)}) copy-start(f32[1,8,80,32]{2,3,1,0:T(8,128)S(1)} %get-tuple-element.172) | copy-start | bytes 245764
  83.4 4.9 %copy-start.3 = (f32[1,8,80,32]{2,3,1,0:T(8,128)}, f32[1,8,80,32]{2,3,1,0:T(8,128)S(1)}, u32[]{:S(2)}) copy-start(f32[1,8,80,32]{2,3,1,0:T(8,128)S(1)} %get-tuple-element.154) | copy-start | bytes 245764
  83.4 4.8 %collective-permute-start.3 = (f32[1,2,1,80,32]{3,4,2,1,0:T(8,128)S(1)}, f32[1,2,1,80,32]{3,4,2,1,0:T(8,128)S(1)}, u32[]{:S(2)}, u32[]{:S(2)}) collective-permute-start(f32[1,2,1,80,32]{3,4,2,1,0:T(8,128)S(1)} %pad_maximum_fusion.1), channel_id=1, source_target_pairs={{0,2},{1,3},{4,6},{5,7},{8,10},{9,11},{12,14},{13,15},{16,18},{17,... | collective-permute-start | bytes 61448 | tf_op jit(solution)/shard_map/ppermute | solution.py:22
  87.0 19.8 %collective-permute-start.5 = (f32[1,1,1,80,32]{3,4,2,1,0:T(8,128)S(1)}, f32[1,1,1,80,32]{3,4,2,1,0:T(8,128)S(1)}, u32[]{:S(2)}, u32[]{:S(2)}) collective-permute-start(f32[1,1,1,80,32]{3,4,2,1,0:T(8,128)S(1)} %slice.841), channel_id=1, source_target_pairs={{2,0},{3,1},{6,4},{7,5},{10,8},{11,9},{14,12},{15,13},{18,16},{19,... | collective-permute-start | bytes 30728 | tf_op jit(solution)/shard_map/ppermute | solution.py:22
  96.3 10.5 %collective-permute-start.8 = (f32[1,2,1,80,32]{3,4,2,1,0:T(8,128)S(1)}, f32[1,2,1,80,32]{3,4,2,1,0:T(8,128)S(1)}, u32[]{:S(2)}, u32[]{:S(2)}) collective-permute-start(f32[1,2,1,80,32]{3,4,2,1,0:T(8,128)S(1)} %pad_add_fusion.4), channel_id=1, source_target_pairs={{0,2},{1,3},{4,6},{5,7},{8,10},{9,11},{12,14},{13,15},{16,18},{17,... | collective-permute-start | bytes 61448 | tf_op jit(solution)/shard_map/ppermute | solution.py:22
  100.4 4.5 %collective-permute-start.7 = (f32[1,1,1,80,32]{3,4,2,1,0:T(8,128)S(1)}, f32[1,1,1,80,32]{3,4,2,1,0:T(8,128)S(1)}, u32[]{:S(2)}, u32[]{:S(2)}) collective-permute-start(f32[1,1,1,80,32]{3,4,2,1,0:T(8,128)S(1)} %slice_bitcast_fusion.26), channel_id=1, source_target_pairs={{2,0},{3,1},{6,4},{7,5},{10,8},{11,9},{14,12},{15,13},{18,16},{19,... | collective-permute-start | bytes 30728 | tf_op jit(solution)/shard_map/ppermute | solution.py:22
  102.1 4.7 %copy-start.4 = (f32[1,8,80,32]{2,3,1,0:T(8,128)S(1)}, f32[1,8,80,32]{2,3,1,0:T(8,128)}, u32[]{:S(2)}) copy-start(f32[1,8,80,32]{2,3,1,0:T(8,128)} %copy-done.3) | copy-start | bytes 245764
  102.1 4.7 %copy-start.6 = (f32[1,8,80,32]{2,3,1,0:T(8,128)S(1)}, f32[1,8,80,32]{2,3,1,0:T(8,128)}, u32[]{:S(2)}) copy-start(f32[1,8,80,32]{2,3,1,0:T(8,128)} %copy-done.5) | copy-start | bytes 245764
  102.2 4.7 %copy-start.15 = (f32[1,8,80,32]{2,3,1,0:T(8,128)S(1)}, f32[1,8,80,32]{2,3,1,0:T(8,128)}, u32[]{:S(2)}) copy-start(f32[1,8,80,32]{2,3,1,0:T(8,128)} %copy-done.14) | copy-start | bytes 245764
  102.2 4.7 %copy-start.36 = (f32[1,8,79,32]{2,3,1,0:T(8,128)S(1)}, f32[1,8,79,32]{2,3,1,0:T(8,128)}, u32[]{:S(2)}) copy-start(f32[1,8,79,32]{2,3,1,0:T(8,128)} %slice.849) | copy-start | bytes 242692
  102.2 4.7 %copy-start.58 = (f32[1,7,80,32]{2,3,1,0:T(8,128)S(1)}, f32[1,7,80,32]{2,3,1,0:T(8,128)}, u32[]{:S(2)}) copy-start(f32[1,7,80,32]{2,3,1,0:T(8,128)} %slice.847) | copy-start | bytes 215044
  102.2 4.7 %copy-start.59 = (f32[1,7,80,32]{2,3,1,0:T(8,128)S(1)}, f32[1,7,80,32]{2,3,1,0:T(8,128)}, u32[]{:S(2)}) copy-start(f32[1,7,80,32]{2,3,1,0:T(8,128)} %slice.840) | copy-start | bytes 215044
  106.8 13.1 %copy-start.2 = (f32[1,9,8,80,32]{3,4,2,1,0:T(8,128)}, f32[1,9,8,80,32]{3,4,2,1,0:T(8,128)S(1)}, u32[]{:S(2)}) copy-start(f32[1,9,8,80,32]{3,4,2,1,0:T(8,128)S(1)} %fusion.68) | copy-start | bytes 2211844
  111.8 20.4 %collective-permute-start.11 = (f32[1,2,1,80,32]{3,4,2,1,0:T(8,128)S(1)}, f32[1,2,1,80,32]{3,4,2,1,0:T(8,128)S(1)}, u32[]{:S(2)}, u32[]{:S(2)}) collective-permute-start(f32[1,2,1,80,32]{3,4,2,1,0:T(8,128)S(1)} %pad_maximum_fusion), channel_id=1, source_target_pairs={{2,0},{3,1},{6,4},{7,5},{10,8},{11,9},{14,12},{15,13},{18,16},{19,... | collective-permute-start | bytes 61448 | tf_op jit(solution)/shard_map/ppermute | solution.py:22
  113.1 7.2 %collective-permute-start.9 = (f32[1,2,1,80,32]{3,4,2,1,0:T(8,128)S(1)}, f32[1,2,1,80,32]{3,4,2,1,0:T(8,128)S(1)}, u32[]{:S(2)}, u32[]{:S(2)}) collective-permute-start(f32[1,2,1,80,32]{3,4,2,1,0:T(8,128)S(1)} %pad_add_fusion.3), channel_id=1, source_target_pairs={{2,0},{3,1},{6,4},{7,5},{10,8},{11,9},{14,12},{15,13},{18,16},{19,... | collective-permute-start | bytes 61448 | tf_op jit(solution)/shard_map/ppermute | solution.py:22
  114.4 5.9 %collective-permute-start.10 = (f32[1,1,1,80,32]{3,4,2,1,0:T(8,128)S(1)}, f32[1,1,1,80,32]{3,4,2,1,0:T(8,128)S(1)}, u32[]{:S(2)}, u32[]{:S(2)}) collective-permute-start(f32[1,1,1,80,32]{3,4,2,1,0:T(8,128)S(1)} %slice_bitcast_fusion.21), channel_id=1, source_target_pairs={{0,2},{1,3},{4,6},{5,7},{8,10},{9,11},{12,14},{13,15},{16,18},{17,... | collective-permute-start | bytes 30728 | tf_op jit(solution)/shard_map/ppermute | solution.py:22
  118.4 8.9 %collective-permute-start.6 = (f32[1,1,1,80,32]{3,4,2,1,0:T(8,128)S(1)}, f32[1,1,1,80,32]{3,4,2,1,0:T(8,128)S(1)}, u32[]{:S(2)}, u32[]{:S(2)}) collective-permute-start(f32[1,1,1,80,32]{3,4,2,1,0:T(8,128)S(1)} %slice.844), channel_id=1, source_target_pairs={{0,2},{1,3},{4,6},{5,7},{8,10},{9,11},{12,14},{13,15},{16,18},{17,... | collective-permute-start | bytes 30728 | tf_op jit(solution)/shard_map/ppermute | solution.py:22
  132.3 10.1 %copy-start.20 = (f32[1,8,80,32]{2,3,1,0:T(8,128)S(1)}, f32[1,8,80,32]{2,3,1,0:T(8,128)}, u32[]{:S(2)}) copy-start(f32[1,8,80,32]{2,3,1,0:T(8,128)} %get-tuple-element.176) | copy-start | bytes 245764
  132.3 10.1 %copy-start.22 = (f32[1,8,80,32]{2,3,1,0:T(8,128)S(1)}, f32[1,8,80,32]{2,3,1,0:T(8,128)}, u32[]{:S(2)}) copy-start(f32[1,8,80,32]{2,3,1,0:T(8,128)} %copy-done.21) | copy-start | bytes 245764
  132.3 10.1 %copy-start.24 = (f32[1,8,80,32]{2,3,1,0:T(8,128)S(1)}, f32[1,8,80,32]{2,3,1,0:T(8,128)}, u32[]{:S(2)}) copy-start(f32[1,8,80,32]{2,3,1,0:T(8,128)} %copy-done.23) | copy-start | bytes 245764
  135.9 11.9 %collective-permute-start.13 = (f32[1,2,1,80,32]{3,4,2,1,0:T(8,128)}, f32[1,2,1,80,32]{3,4,2,1,0:T(8,128)}, u32[]{:S(2)}, u32[]{:S(2)}) collective-permute-start(f32[1,2,1,80,32]{3,4,2,1,0:T(8,128)} %pad_add_fusion.2), channel_id=1, source_target_pairs={{0,2},{1,3},{4,6},{5,7},{8,10},{9,11},{12,14},{13,15},{16,18},{17,... | collective-permute-start | bytes 61448 | tf_op jit(solution)/shard_map/ppermute | solution.py:22
  141.0 4.8 %collective-permute-start.12 = (f32[1,1,1,80,32]{3,4,2,1,0:T(8,128)}, f32[1,1,1,80,32]{3,4,2,1,0:T(8,128)S(1)}, u32[]{:S(2)}, u32[]{:S(2)}) collective-permute-start(f32[1,1,1,80,32]{3,4,2,1,0:T(8,128)} %slice_bitcast_fusion.18), channel_id=1, source_target_pairs={{2,0},{3,1},{6,4},{7,5},{10,8},{11,9},{14,12},{15,13},{18,16},{19,... | collective-permute-start | bytes 30728 | tf_op jit(solution)/shard_map/ppermute | solution.py:22
  144.0 4.5 %copy-start.34 = (f32[1,8,80,32]{2,3,1,0:T(8,128)S(1)}, f32[1,8,80,32]{2,3,1,0:T(8,128)}, u32[]{:S(2)}) copy-start(f32[1,8,80,32]{2,3,1,0:T(8,128)} %get-tuple-element.234) | copy-start | bytes 245764
  144.0 4.5 %copy-start.35 = (f32[1,8,80,32]{2,3,1,0:T(8,128)S(1)}, f32[1,8,80,32]{2,3,1,0:T(8,128)}, u32[]{:S(2)}) copy-start(f32[1,8,80,32]{2,3,1,0:T(8,128)} %get-tuple-element.236) | copy-start | bytes 245764
  144.0 4.5 %copy-start.37 = (f32[1,8,80,32]{2,3,1,0:T(8,128)S(1)}, f32[1,8,80,32]{2,3,1,0:T(8,128)}, u32[]{:S(2)}) copy-start(f32[1,8,80,32]{2,3,1,0:T(8,128)} %get-tuple-element.161) | copy-start | bytes 245764
  144.0 4.5 %copy-start.38 = (f32[1,8,80,32]{2,3,1,0:T(8,128)S(1)}, f32[1,8,80,32]{2,3,1,0:T(8,128)}, u32[]{:S(2)}) copy-start(f32[1,8,80,32]{2,3,1,0:T(8,128)} %get-tuple-element.159) | copy-start | bytes 245764
  152.3 5.4 %copy-start.71 = (pred[4,16]{1,0:T(4,128)(4,1)S(1)}, pred[4,16]{1,0:T(4,128)(4,1)}, u32[]{:S(2)}) copy-start(pred[4,16]{1,0:T(4,128)(4,1)} %copy-done.70) | copy-start | bytes 196
  153.2 13.3 %all-to-all-start.1 = ((f32[4,16,3,640]{3,1,2,0:T(8,128)}), f32[4,16,3,640]{3,1,2,0:T(8,128)S(1)}, u32[]{:S(2)}, u32[]{:S(2)}) async-start(f32[4,16,3,640]{3,1,2,0:T(8,128)} %copy_select_fusion), calls=%async_computation.1 | async-start | bytes 983040 | tf_op jit(solution)/shard_map/all_to_all | solution.py:196
  157.7 46.4 %copy-start.63 = (f32[32,3,640]{2,0,1:T(8,128)S(1)}, f32[32,3,640]{2,0,1:T(8,128)}, u32[]{:S(2)}) copy-start(f32[32,3,640]{2,0,1:T(8,128)} %param.33) | copy-start | bytes 737284
  157.7 46.4 %all-reduce.87.cloned.1.call-start = ((), (), s32[]{:S(2)}) async-start(), calls=%async_computation.2 | async-start | bytes 491520 | tf_op jit(solution)/shard_map/psum | solution.py:209
  (50 other events, 122.2 us)
Sparse Core Ops, SparseCore 0:
  167.9 36.1 all-reduce.86
where the time goes:
time: 215 us; the launch traced here: 213 us
  local copies, waits for them, and re-layouts  65.7 us (31%)
  waiting for transfers between devices  48.2 us (22%)
  starting transfers between devices  41.2 us (19%)
  other arithmetic  40.2 us (19%)
  between operations  16.5 us (8%)
    psum x1, waiting for transfers between devices, on_device(): total = lax.psum(partial_sum, ('sub', 'rep'))  36.3 us
    ppermute x14, starting transfers between devices, passed_along(): return lax.ppermute(block, axis, route)  31.2 us
    all_to_all x1, waiting for transfers between devices, on_device(): lax.all_to_all(returning, 'shot', split_axis=0, concat_axis=0, tiled=True)  8.69 us
    all_to_all x1, starting transfers between devices, on_device(): lax.all_to_all(outgoing, 'shot', split_axis=0, concat_axis=0, tiled=True)  5.42 us
    slice x6, local copies, waits for them, and re-layouts, plus_y(): field[:, :, 1:]  4.53 us
    all_to_all x1, starting transfers between devices, on_device(): lax.all_to_all(returning, 'shot', split_axis=0, concat_axis=0, tiled=True)  4.53 us
  transfers between devices with their start and end apart: 17, of which 4 were waited for; matrix products, arithmetic and copies ran while one was open for 36% of the time, Pallas kernels for 0%

commit v1 on v0

v1 whole, which is shorter than its diff:
```python
import functools
import jax
import jax.numpy as jnp
from jax import lax
from jax.experimental import pallas as pl
from jax.experimental.pallas import tpu as pltpu
from jax.sharding import PartitionSpec as P

DEPTH = 32
TILE_X = 4
TILE_Y = 5
SLAB_XT = 2
SLAB_YT = 16
NSTEPS = 2
SLAB_TILES = 32
LX = SLAB_XT * TILE_X
WY = SLAB_YT * TILE_Y
LANES = 128

time_step = 0.18
learn_rate = 0.5
MESH = pl.DeviceIdType.MESH
F32 = jnp.float32

TO_PRIOR = (2, 2, 1, 4, 1)
TO_NEXT = (4, 1, 2, 2, 2)


def next_y(f):
    return pltpu.roll(f, LANES - 1, 1)


def prior_y(f):
    return pltpu.roll(f, 1, 1)


def physics(
    start_ref, adj_ref, par_ref, wave_ref, src_ref, rec_ref, obs_ref, grad_ref,
    F, C, W, A, B, DV, ST, CNT, OB, R0,
    send_l, send_r, recv_l, recv_r, ss_l, ss_r, rs_l, rs_r,
):
    n_sub = lax.axis_size("sub")
    me = lax.axis_index("sub")
    has_l = me > 0
    has_r = me < n_sub - 1
    left = {"sub": jnp.maximum(me - 1, 0)}
    right = {"sub": jnp.minimum(me + 1, n_sub - 1)}
    barrier = pltpu.get_barrier_semaphore()

    @pl.when(has_l)
    def _():
        pl.semaphore_signal(barrier, inc=1, device_id=left, device_id_type=MESH)

    @pl.when(has_r)
    def _():
        pl.semaphore_signal(barrier, inc=1, device_id=right, device_id_type=MESH)

    @pl.when(has_l)
    def _():
        pl.semaphore_wait(barrier, 1)

    @pl.when(has_r)
    def _():
        pl.semaphore_wait(barrier, 1)

    def copies(e):
        nl, nr = TO_PRIOR[e], TO_NEXT[e]
        to_l = pltpu.make_async_remote_copy(
            src_ref=send_l.at[e, pl.ds(0, nl)], dst_ref=recv_r.at[e, pl.ds(0, nl)],
            send_sem=ss_l.at[e], recv_sem=rs_r.at[e], device_id=left, device_id_type=MESH)
        to_r = pltpu.make_async_remote_copy(
            src_ref=send_r.at[e, pl.ds(0, nr)], dst_ref=recv_l.at[e, pl.ds(0, nr)],
            send_sem=ss_r.at[e], recv_sem=rs_l.at[e], device_id=right, device_id_type=MESH)
        return to_l, to_r

    def send(e, firsts, lasts):
        to_l, to_r = copies(e)

        @pl.when(has_l)
        def _():
            for k, (ref, i) in enumerate(firsts):
                send_l[e, k] = ref[i, 1]
            to_l.start()

        @pl.when(has_r)
        def _():
            for k, (ref, i) in enumerate(lasts):
                send_r[e, k] = ref[i, LX]
            to_r.start()

    def receive(e, firsts, lasts):
        to_l, to_r = copies(e)

        @pl.when(has_r)
        def _():
            to_r.wait_send()
            to_l.wait_recv()
            for k, (ref, i) in enumerate(firsts):
                ref[i, LX + 1] = recv_r[e, k]

        @pl.when(has_l)
        def _():
            to_l.wait_send()
            to_r.wait_recv()
            for k, (ref, i) in enumerate(lasts):
                ref[i, 0] = recv_l[e, k]

    zrow = lax.broadcasted_iota(jnp.int32, (DEPTH, LANES), 0)
    lane = lax.broadcasted_iota(jnp.int32, (DEPTH, LANES), 1)
    inside = lane < WY

    def next_z(f):
        return jnp.where(zrow == DEPTH - 1, 0.0, pltpu.roll(f, DEPTH - 1, 0))

    def prior_z(f):
        return jnp.where(zrow == 0, 0.0, pltpu.roll(f, 1, 0))

    def py(f):
        return next_y(f) - f

    def my(f):
        return f - prior_y(f)

    def pz(f):
        return next_z(f) - f

    def mz(f):
        return f - prior_z(f)

    def px(ref, i, x):
        return ref[i, x + 1] - ref[i, x]

    def mx(ref, i, x):
        return ref[i, x] - ref[i, x - 1]

    zero = jnp.zeros((DEPTH, LANES), F32)

    def strain_cot(x, c):
        lame = par_ref[0, x - 1]
        shear = par_ref[1, x - 1]
        trace = time_step * lame * (c[0] + c[1] + c[2])
        ds = time_step * shear
        W[0, x] = trace + 2.0 * ds * c[0]
        W[1, x] = trace + 2.0 * ds * c[1]
        W[2, x] = trace + 2.0 * ds * c[2]
        W[3, x] = ds * c[3]
        W[4, x] = ds * c[4]
        W[5, x] = ds * c[5]

    def edges_first(body, after):
        body(1)
        body(LX)
        after()
        lax.fori_loop(2, LX, lambda x, _: (body(x), 0)[1], 0)

    for i in range(9):
        F[i, 0] = zero
        F[i, LX + 1] = zero
    for i in range(6):
        W[i, 0] = zero
        W[i, LX + 1] = zero
    for i in range(3):
        A[i, 0] = zero
        A[i, LX + 1] = zero

    def load(x):
        for i in range(9):
            F[i, x] = zero
            F[i, x, :, pl.ds(0, WY)] = start_ref[i, x - 1].astype(F32)
            C[i, x - 1] = zero
            C[i, x - 1, :, pl.ds(0, WY)] = adj_ref[i, x - 1].astype(F32)
        B[x - 1] = jnp.where(inside, 1.0 / jnp.where(inside, par_ref[2, x - 1], 1.0), 0.0)
        strain_cot(x, [C[3 + i, x - 1] for i in range(6)])

    e0 = ([(F, 3), (W, 0)], [(F, 6), (F, 7), (W, 3), (W, 4)])
    e1 = ([(F, 1), (F, 2)], [(F, 0)])
    e2 = ([(F, 3)], [(F, 6), (F, 7)])
    e3 = ([(F, 1), (F, 2), (A, 1), (A, 2)], [(F, 0), (A, 0)])
    e4 = ([(W, 0)], [(W, 3), (W, 4)])

    edges_first(load, lambda: send(0, *e0))

    cell = rec_ref[...]
    q = cell >> 5
    rx = (q * 52429) >> 22
    ry = q - rx * WY
    rrow = (rx - me * LX) * DEPTH + (cell & (DEPTH - 1))
    nrec = rec_ref.shape[1]
    rows = lax.broadcasted_iota(jnp.int32, (LX * DEPTH, nrec), 0)
    cols = lax.broadcasted_iota(jnp.int32, (LANES, nrec), 0)
    at_row = jnp.where(rows == rrow, 1.0, 0.0).astype(F32)
    at_col = cols == ry
    dims = (((1,), (1,)), ((), ()))

    def spread(values):
        return lax.dot_general(
            at_row, jnp.where(at_col, values, 0.0), dims,
            precision=lax.Precision.HIGHEST, preferred_element_type=F32)

    CNT[...] = spread(jnp.ones((1, nrec), F32)).reshape(LX, DEPTH, LANES)
    OB[0] = spread(obs_ref[0:1]).reshape(LX, DEPTH, LANES)
    OB[1] = spread(obs_ref[1:2]).reshape(LX, DEPTH, LANES)

    scell = src_ref[0]
    sq = scell >> 5
    sx = (sq * 52429) >> 22
    sy = sq - sx * WY
    sz = scell & (DEPTH - 1)
    at_src = jnp.where((zrow == sz) & (lane == sy), 1.0, 0.0)

    def divergence(x):
        return [
            px(F, 3, x) + my(F[6, x]) + mz(F[7, x]),
            mx(F, 6, x) + py(F[4, x]) + mz(F[8, x]),
            mx(F, 7, x) + my(F[8, x]) + pz(F[5, x]),
        ]

    def strains(x):
        vx, vy, vz = F[0, x], F[1, x], F[2, x]
        return [
            mx(F, 0, x), my(vy), mz(vz),
            py(vx) + px(F, 1, x), pz(vx) + px(F, 2, x), pz(vy) + py(vz),
        ]

    def velocity_cot(x):
        exx, eyy, ezz = W[0, x], W[1, x], W[2, x]
        gxy, gxz, gyz = W[3, x], W[4, x], W[5, x]
        return [
            px(W, 0, x) + my(gxy) + mz(gxz),
            py(eyy) + mx(W, 3, x) + mz(gyz),
            pz(ezz) + mx(W, 4, x) + my(gyz),
        ]

    def first_velocity(x):
        b = time_step * B[x - 1]
        d = divergence(x)
        for i in range(3):
            DV[i, x - 1] = d[i]
            F[i, x] = F[i, x] + b * d[i]
        R0[x - 1] = CNT[x - 1] * F[2, x] - OB[0, x - 1]

    receive(0, *e0)
    edges_first(first_velocity, lambda: send(1, *e1))

    def first_stress(x):
        lame = time_step * par_ref[0, x - 1]
        shear = time_step * par_ref[1, x - 1]
        s = strains(x)
        for i in range(6):
            ST[i, x - 1] = s[i]
        amp = jnp.where(x - 1 + me * LX == sx, time_step * wave_ref[0], 0.0)
        base = lame * (s[0] + s[1] + s[2]) + amp * at_src
        for i in range(3):
            F[3 + i, x] = F[3 + i, x] + (base + 2.0 * shear * s[i])
            F[6 + i, x] = F[6 + i, x] + shear * s[3 + i]

    receive(1, *e1)
    edges_first(first_stress, lambda: send(2, *e2))

    def second_velocity(x):
        inv = B[x - 1]
        b = time_step * inv
        d = divergence(x)
        w = velocity_cot(x)
        for i in range(3):
            F[i, x] = F[i, x] + b * d[i]
        res = CNT[x - 1] * F[2, x] - OB[1, x - 1]
        total = zero
        for i in range(3):
            c = C[i, x - 1] - w[i]
            if i == 2:
                c = c + res
            C[i, x - 1] = c
            a = b * c
            A[i, x] = a
            total = total + a * d[i]
        grad_ref[2, x - 1] = -inv * total

    receive(2, *e2)
    edges_first(second_velocity, lambda: send(3, *e3))

    def model_part(c, s):
        part_lame = (s[0] + s[1] + s[2]) * (c[0] + c[1] + c[2])
        part_shear = 2.0 * (s[0] * c[0] + s[1] * c[1] + s[2] * c[2]) + (
            s[3] * c[3] + s[4] * c[4] + s[5] * c[5])
        return part_lame, part_shear

    def stress_back(x):
        c = [C[3 + i, x - 1] for i in range(6)]
        lame1, shear1 = model_part(c, strains(x))
        ax, ay, az = A[0, x], A[1, x], A[2, x]
        c = [
            c[0] - mx(A, 0, x),
            c[1] - my(ay),
            c[2] - mz(az),
            c[3] - py(ax) - px(A, 1, x),
            c[4] - pz(ax) - px(A, 2, x),
            c[5] - pz(ay) - py(az),
        ]
        strain_cot(x, c)
        lame0, shear0 = model_part(c, [ST[i, x - 1] for i in range(6)])
        grad_ref[0, x - 1] = time_step * (lame1 + lame0)
        grad_ref[1, x - 1] = time_step * (shear1 + shear0)

    receive(3, *e3)
    edges_first(stress_back, lambda: send(4, *e4))

    def last_velocity(x):
        inv = B[x - 1]
        b = time_step * inv
        w = velocity_cot(x)
        total = zero
        for i in range(3):
            c = C[i, x - 1] - w[i]
            if i == 2:
                c = c + R0[x - 1]
            total = total + b * c * DV[i, x - 1]
        grad_ref[2, x - 1] = grad_ref[2, x - 1] - inv * total

    receive(4, *e4)
    lax.fori_loop(1, LX + 1, lambda x, _: (last_velocity(x), 0)[1], 0)


def run_physics(start, adj, params, wave, src, rec, obs):
    vm = pl.BlockSpec(memory_space=pltpu.VMEM)
    sm = pl.BlockSpec(memory_space=pltpu.SMEM)
    layer = (DEPTH, LANES)
    halo = pltpu.VMEM((5, 4) + layer, F32)
    dma = pltpu.SemaphoreType.DMA((5,))
    return pl.pallas_call(
        physics,
        out_shape=jax.ShapeDtypeStruct((3, LX) + layer, F32),
        in_specs=[vm, vm, vm, sm, sm, vm, vm],
        out_specs=vm,
        scratch_shapes=[
            pltpu.VMEM((9, LX + 2) + layer, F32),
            pltpu.VMEM((9, LX) + layer, F32),
            pltpu.VMEM((6, LX + 2) + layer, F32),
            pltpu.VMEM((3, LX + 2) + layer, F32),
            pltpu.VMEM((LX,) + layer, F32),
            pltpu.VMEM((3, LX) + layer, F32),
            pltpu.VMEM((6, LX) + layer, F32),
            pltpu.VMEM((LX,) + layer, F32),
            pltpu.VMEM((2, LX) + layer, F32),
            pltpu.VMEM((LX,) + layer, F32),
            halo, halo, halo, halo, dma, dma, dma, dma,
        ],
        compiler_params=pltpu.CompilerParams(
            collective_id=0, has_side_effects=True, vmem_limit_bytes=40 * 1024 * 1024),
    )(start, adj, params, wave, src, rec, obs)


def on_device(
    model,
    accum,
    owner_map,
    aperture,
    start_state,
    adjoint_end,
    wavelet,
    source_cell,
    receiver_cell,
    observed,
):
    n_shot = lax.axis_size("shot")
    my_shot = lax.axis_index("shot")
    tiles_dev = model.shape[0]
    tile_cells = model.shape[2]
    per_owner = 2 * SLAB_TILES // n_shot
    slab_slots = owner_map[aperture[:, 0, :]]
    owners = slab_slots // tiles_dev
    local_rows = slab_slots % tiles_dev
    positions = jnp.arange(SLAB_TILES, dtype=jnp.int32)
    earlier = (owners[:, :, None] == owners[:, None, :]) & (
        positions[None, None, :] < positions[None, :, None]
    )
    ranks = jnp.sum(earlier.astype(jnp.int32), axis=2)
    slot_ids = jnp.arange(per_owner, dtype=jnp.int32)
    serve = (owners[:, None, :] == my_shot) & (ranks[:, None, :] == slot_ids[None, :, None])
    served = jnp.any(serve, axis=2)
    serve_rows = jnp.sum(jnp.where(serve, local_rows[:, None, :], 0), axis=2)
    outgoing = jnp.where(served[:, :, None, None], model[serve_rows], 0.0)
    incoming = lax.all_to_all(outgoing, "shot", split_axis=0, concat_axis=0, tiled=True)
    my_owners = owners[my_shot]
    my_ranks = ranks[my_shot]
    slab = incoming.reshape(n_shot * per_owner, 3, tile_cells)[my_owners * per_owner + my_ranks]
    slab_x = SLAB_XT * TILE_X
    slab_y = SLAB_YT * TILE_Y
    params = slab.reshape(SLAB_XT, SLAB_YT, 3, TILE_X, TILE_Y, DEPTH)
    params = params.transpose(2, 0, 3, 5, 1, 4).reshape(3, slab_x, DEPTH, slab_y)
    params = jnp.pad(params, ((0, 0), (0, 0), (0, 0), (0, LANES - slab_y)))
    start = start_state[0, 0, 0].transpose(0, 1, 3, 2)
    adj = adjoint_end[0, 0, 0].transpose(0, 1, 3, 2)
    gradient = run_physics(
        start, adj, params, wavelet.reshape(NSTEPS), source_cell.reshape(1),
        receiver_cell.reshape(1, -1), observed[0, 0, 0],
    )[..., :slab_y]
    back = gradient.reshape(3, SLAB_XT, TILE_X, DEPTH, SLAB_YT, TILE_Y)
    back = back.transpose(1, 4, 0, 2, 5, 3).reshape(SLAB_TILES, 3, tile_cells)
    all_slots = jnp.arange(per_owner, dtype=jnp.int32)
    owner_ids = jnp.arange(n_shot, dtype=jnp.int32)
    place = (my_owners[None, None, :] == owner_ids[:, None, None]) & (
        my_ranks[None, None, :] == all_slots[None, :, None]
    )
    placed = jnp.any(place, axis=2)
    place_rows = jnp.sum(jnp.where(place, positions[None, None, :], 0), axis=2)
    returning = jnp.where(placed[:, :, None, None], back[place_rows], 0.0)
    arrived = lax.all_to_all(returning, "shot", split_axis=0, concat_axis=0, tiled=True)
    pick = (
        serve_rows[:, :, None] == jnp.arange(tiles_dev, dtype=jnp.int32)[None, None, :]
    ) & served[:, :, None]
    pick = pick.astype(jnp.float32).reshape(n_shot * per_owner, tiles_dev)
    partial_sum = jnp.einsum(
        "sd,sc->dc",
        pick,
        arrived.reshape(n_shot * per_owner, 3 * tile_cells),
        precision=lax.Precision.HIGHEST,
        preferred_element_type=jnp.float32,
    )
    partial_sum = partial_sum.reshape(tiles_dev, 3, tile_cells)
    total = lax.psum(partial_sum, ("sub", "rep"))
    new_accum = accum + total * total
    new_model = model - learn_rate * total / jnp.sqrt(new_accum)
    return (new_model, new_accum)


def solution(mesh):
    in_specs = (
        P(("groups", "shot"), None, None),
        P(("groups", "shot"), None, None),
        P("groups"),
        P("groups", "sub", None),
        P(("groups", "shot"), "rep", None, None, "sub", None, None),
        P(("groups", "shot"), "rep", None, None, "sub", None, None),
        P(("groups", "shot"), "rep", None, None),
        P(("groups", "shot"), "rep", None),
        P(("groups", "shot"), "rep", None, None),
        P(("groups", "shot"), "rep", None, None, None),
    )
    out_specs = (P(("groups", "shot"), None, None), P(("groups", "shot"), None, None))
    return jax.shard_map(
        on_device, mesh=mesh, in_specs=in_specs, out_specs=out_specs, check_vma=False
    )
```

time: 215 us -> 111 us (0.52)
  local copies, waits for them, and re-layouts: 65.7 us -> 8.26 us
  other arithmetic: 40.2 us -> 5.28 us
  starting transfers between devices: 41.2 us -> 9.06 us
  Pallas kernels: 0 us -> 13.6 us
  waiting for transfers between devices: 48.2 us -> 57.2 us
    ppermute x14 -> x0, starting transfers between devices: 31.2 us -> none  [passed_along(): return lax.ppermute(block, axis, route)]
    slice x35 -> x1, local copies, waits for them, and re-layouts: 21.8 us -> 0.37 us  [on_device(): run_physics(start, adj, params, wavelet.reshape(NSTEPS), source_cell.resh...]
    pallas_call x0 -> x1, Pallas kernels: none -> 13.6 us  [run_physics(): pl.pallas_call(physics, out_shape=jax.ShapeDtypeStruct((3, LX) + layer, F...]
    all_to_all x1, waiting for transfers between devices: 0.01 us -> 12.2 us  [on_device(): lax.all_to_all(outgoing, 'shot', split_axis=0, concat_axis=0, tiled=True)]
    add x8 -> x0, other arithmetic: 11.5 us -> none  [the longest x2 2.59 us: velocity_half(): vel_z + time_step * buoyancy * (minus_x(stress_xz, left_rim[:, 1]) + minu...]
    scatter-add x8 -> x0, other arithmetic: 8.54 us -> none  [the longest x2 3.94 us: on_device(): flat_vz = cotangent[:, 2].reshape(shots, cells).at[shot_rows, receiver_ro...]
    another operation x12 -> x0, local copies, waits for them, and re-layouts: 7.27 us -> none
    mul x6 -> x0, local copies, waits for them, and re-layouts: 6.87 us -> none  [the longest x2 2.95 us: stress_half(): time_step * shear * (plus_y(vel_x) + plus_x(vel_y, right_rim[:, 0]))]
  transfers between devices with their start and end apart: 17 -> 3, of which waited for: 4 -> 3; matrix products, arithmetic and copies ran while one was open for 36% -> 0% of each run, Pallas kernels for 0% -> 0%
where the time goes in v1:
time: 111 us; the launch traced here: 109 us
  waiting for transfers between devices  57.2 us (52%)
  between operations  14.9 us (13%)
  Pallas kernels  13.6 us (12%)
  starting transfers between devices  9.06 us (8%)
  local copies, waits for them, and re-layouts  8.26 us (7%)
  other arithmetic  5.28 us (5%)
    psum x1, waiting for transfers between devices, on_device(): total = lax.psum(partial_sum, ('sub', 'rep'))  36.3 us
    pallas_call x1, Pallas kernels, run_physics(): pl.pallas_call(physics, out_shape=jax.ShapeDtypeStruct((3, LX) + layer, F...  13.6 us
    all_to_all x1, waiting for transfers between devices, on_device(): lax.all_to_all(outgoing, 'shot', split_axis=0, concat_axis=0, tiled=True)  12.2 us
    all_to_all x1, waiting for transfers between devices, on_device(): lax.all_to_all(returning, 'shot', split_axis=0, concat_axis=0, tiled=True)  8.64 us
    all_to_all x1, starting transfers between devices, on_device(): lax.all_to_all(outgoing, 'shot', split_axis=0, concat_axis=0, tiled=True)  5.42 us
    all_to_all x1, starting transfers between devices, on_device(): lax.all_to_all(returning, 'shot', split_axis=0, concat_axis=0, tiled=True)  3.6 us
  transfers between devices with their start and end apart: 3, of which 3 were waited for; matrix products, arithmetic and copies ran while one was open for 0% of the time, Pallas kernels for 0%

profile of v1, /device:TPU:1, one launch (start us, length us, event | category | flops | bytes accessed | tf_op | source)
XLA Modules:
  0.0 109.3 jit_solution(16756726156024640980)
XLA Ops:
  7.2 0.0 copy-start
  7.2 0.0 copy-start.6
  7.2 0.7 compare_select_fusion.2
  8.0 0.1 reshape.307
  8.1 0.0 copy-done
  8.1 1.2 %gather_fusion = s32[128]{0:T(128)S(1)} fusion(s32[128]{0:T(128)S(1)} %copy-done, s32[1024]{0:T(1024)S(1)} %pad_clamp_fusion.3), kind=kCustom, calls=%fused_computation | custom fusion | bytes 1536 | tf_op jit(solution)/shard_map/gather | solution.py:370
  9.3 0.1 reshape.306
  9.4 0.2 convert_reduce_fusion
  9.6 0.2 fusion.5
  9.8 0.2 select_reduce_fusion
  9.9 0.1 reshape.315
  10.0 0.0 copy-done.6
  10.0 1.3 %gather_fusion.1 = f32[64,3,640]{2,0,1:T(8,128)S(1)} fusion(f32[32,3,640]{2,0,1:T(8,128)S(1)} %copy-done.6, s32[1024]{0:T(1024)S(1)} %pad_clamp_fusion.2), kind=kCustom, calls=%fused_computation.1 | custom fusion | bytes 983296 | tf_op jit(solution)/shard_map/gather | solution.py:382
  11.4 0.9 copy_select_fusion.1
  12.2 5.4 %all-to-all-start = ((f32[4,16,3,640]{3,1,2,0:T(8,128)}), f32[4,16,3,640]{3,1,2,0:T(8,128)S(1)}, u32[]{:S(2)}, u32[]{:S(2)}) async-start(f32[4,16,3,640]{3,1,2,0:T(8,128)} %copy_select_fusion.1), calls=%async_computation | async-start | bytes 983040 | tf_op jit(solution)/shard_map/all_to_all | solution.py:383
  18.3 0.1 fusion.3
  18.5 0.1 reshape.331
  18.6 0.2 and_reduce_fusion
  18.8 12.2 %all-to-all-done = f32[4,16,3,640]{3,1,2,0:T(8,128)S(1)} async-done(((f32[4,16,3,640]{3,1,2,0:T(8,128)}), f32[4,16,3,640]{3,1,2,0:T(8,128)S(1)}, u32[]{:S(2)}, u32[]{:S(2)}) %all-to-all-start) | async-done | bytes 491552 | tf_op jit(solution)/shard_map/all_to_all | solution.py:383
  30.9 0.3 copy.34
  31.2 0.8 gather_fusion.2
  32.0 0.5 reshape.297
  32.5 0.3 copy.36
  32.7 0.0 copy-start.1
  32.7 0.0 copy-start.2
  32.7 0.0 copy-start.3
  32.8 0.0 copy-start.4
  32.8 0.0 copy-start.5
  32.8 0.3 copy.37
  33.1 0.6 copy-done.1
  33.8 0.2 copy-done.2
  34.0 0.0 copy-done.4
  34.0 13.6 %shard_map.113 = f32[3,8,32,128]{3,2,1,0:T(8,128)S(1)} custom-call(bf16[9,8,32,80]{3,2,1,0:T(8,128)(2,1)S(1)} %bitcast.58, bf16[9,8,32,80]{3,2,1,0:T(8,128)(2,1)S(1)} %bitcast.59, f32[3,8,32,128]{3,2,1,0:T(8,128)S(1)} %pad.4.par_ref, f32[2]{0:T(128)S(1)} %bitcast.62, s32[1]{0:T(128)} %bitcast.56.src_ref, s32[1,256]{1,0:T(1,128)S(1)} %bitcast.61, ...), custom_call_target="tpu_custom_call" | custom-call | tf_op jit(solution)/shard_map/pallas_call | solution.py:330
  47.6 0.4 copy.38
  47.9 0.3 copy.47
  48.2 0.5 reshape.341
  48.8 1.0 gather_fusion.3
  49.7 0.9 copy_select_fusion
  50.6 3.6 %all-to-all-start.1 = ((f32[4,16,3,640]{3,1,2,0:T(8,128)}), f32[4,16,3,640]{3,1,2,0:T(8,128)S(1)}, u32[]{:S(2)}, u32[]{:S(2)}) async-start(f32[4,16,3,640]{3,1,2,0:T(8,128)} %copy_select_fusion), calls=%async_computation.1 | async-start | bytes 983040 | tf_op jit(solution)/shard_map/all_to_all | solution.py:408
  54.2 0.0 all-reduce.3.cloned.1.call-start
  54.3 0.1 fusion.6
  54.4 8.6 %all-to-all-done.1 = f32[4,16,3,640]{3,1,2,0:T(8,128)S(1)} async-done(((f32[4,16,3,640]{3,1,2,0:T(8,128)}), f32[4,16,3,640]{3,1,2,0:T(8,128)S(1)}, u32[]{:S(2)}, u32[]{:S(2)}) %all-to-all-start.1) | async-done | bytes 491552 | tf_op jit(solution)/shard_map/all_to_all | solution.py:408
  63.0 0.3 copy.42
  63.3 1.0 fusion
  64.3 0.0 all-reduce.3.cloned.1.call-update
  64.3 36.3 %all-reduce.3.cloned.1.call-done = f32[32,3,640]{2,0,1:T(8,128)} async-done(((f32[32,3,640]{2,0,1:T(8,128)}), f32[32,3,640]{2,0,1:T(8,128)}) %all-reduce.3.cloned.1.call-update) | async-done | bytes 245776 | tf_op jit(solution)/shard_map/psum | solution.py:421
  100.6 0.0 copy-done.7
  100.6 1.8 %multiply_subtract_fusion = (f32[32,3,640]{2,0,1:T(8,128)}, f32[32,3,640]{2,0,1:T(8,128)}) fusion(f32[32,3,640]{2,0,1:T(8,128)S(1)} %copy-done.6, f32[32,3,640]{2,0,1:T(8,128)} %all-reduce.3.cloned.1.call-done, f32[32,3,640]{2,0,1:T(8,128)S(1)} %copy-done.7), kind=kLoop, calls=%fused_computation.9 | loop fusion | flops 307200 | bytes 1228800 | tf_op jit(solution)/shard_map/sub | solution.py:423
  (18 shorter events, 0.2 us)
Async XLA Ops:
  7.2 0.9 copy-start
  7.2 2.9 %copy-start.6 = (f32[32,3,640]{2,0,1:T(8,128)S(1)}, f32[32,3,640]{2,0,1:T(8,128)}, u32[]{:S(2)}) copy-start(f32[32,3,640]{2,0,1:T(8,128)} %param.10) | copy-start | bytes 737284
  12.2 18.7 %all-to-all-start = ((f32[4,16,3,640]{3,1,2,0:T(8,128)}), f32[4,16,3,640]{3,1,2,0:T(8,128)S(1)}, u32[]{:S(2)}, u32[]{:S(2)}) async-start(f32[4,16,3,640]{3,1,2,0:T(8,128)} %copy_select_fusion.1), calls=%async_computation | async-start | bytes 983040 | tf_op jit(solution)/shard_map/all_to_all | solution.py:383
  32.7 1.1 copy-start.1
  32.7 1.2 %copy-start.2 = (bf16[1,1,1,9,8,80,32]{5,6,4,3,2,1,0:T(8,128)(2,1)S(1)}, bf16[1,1,1,9,8,80,32]{5,6,4,3,2,1,0:T(8,128)(2,1)}, u32[]{:S(2)}) copy-start(bf16[1,1,1,9,8,80,32]{5,6,4,3,2,1,0:T(8,128)(2,1)} %param.15) | copy-start | bytes 1105924
  32.7 1.2 %copy-start.3 = (f32[1,1,1,2,256]{4,3,2,1,0:T(2,128)S(1)}, f32[1,1,1,2,256]{4,3,2,1,0:T(2,128)}, u32[]{:S(2)}) copy-start(f32[1,1,1,2,256]{4,3,2,1,0:T(2,128)} %param.19) | copy-start | bytes 6148
  32.8 1.2 %copy-start.4 = (s32[1,1,1,256]{3,2,1,0:T(1,128)S(1)}, s32[1,1,1,256]{3,2,1,0:T(1,128)}, u32[]{:S(2)}) copy-start(s32[1,1,1,256]{3,2,1,0:T(1,128)} %param.18) | copy-start | bytes 3076
  32.8 1.2 %copy-start.5 = (f32[1,1,1,2]{3,2,1,0:T(1,128)S(1)}, f32[1,1,1,2]{3,2,1,0:T(1,128)}, u32[]{:S(2)}) copy-start(f32[1,1,1,2]{3,2,1,0:T(1,128)} %param.16) | copy-start | bytes 28
  50.6 50.0 %copy-start.7 = (f32[32,3,640]{2,0,1:T(8,128)S(1)}, f32[32,3,640]{2,0,1:T(8,128)}, u32[]{:S(2)}) copy-start(f32[32,3,640]{2,0,1:T(8,128)} %param.11) | copy-start | bytes 737284
  50.6 12.4 %all-to-all-start.1 = ((f32[4,16,3,640]{3,1,2,0:T(8,128)}), f32[4,16,3,640]{3,1,2,0:T(8,128)S(1)}, u32[]{:S(2)}, u32[]{:S(2)}) async-start(f32[4,16,3,640]{3,1,2,0:T(8,128)} %copy_select_fusion), calls=%async_computation.1 | async-start | bytes 983040 | tf_op jit(solution)/shard_map/all_to_all | solution.py:408
  54.2 46.4 %all-reduce.3.cloned.1.call-start = ((), (), s32[]{:S(2)}) async-start(), calls=%async_computation.2 | async-start | bytes 491520 | tf_op jit(solution)/shard_map/psum | solution.py:421
Sparse Core Ops, SparseCore 0:
  64.4 36.1 all-reduce.2

commit v2 on v1

--- a/solution.py
+++ b/solution.py
@@ -1,4 +1,3 @@
-import functools
 import jax
 import jax.numpy as jnp
 from jax import lax
@@ -21,6 +20,10 @@
 learn_rate = 0.5
 MESH = pl.DeviceIdType.MESH
 F32 = jnp.float32
+BF16 = jnp.bfloat16
+TILES = 32
+HALF = 8
+QAC = 3 * TILE_X * DEPTH
 
 TO_PRIOR = (2, 2, 1, 4, 1)
 TO_NEXT = (4, 1, 2, 2, 2)
@@ -34,34 +37,109 @@
     return pltpu.roll(f, 1, 1)
 
 
+def split3(v):
+    hi = v.astype(BF16)
+    rest = v - hi.astype(F32)
+    mid = rest.astype(BF16)
+    return hi, mid, (rest - mid.astype(F32)).astype(BF16)
+
+
+def dot(x, y):
+    return lax.dot_general(x, y, (((1,), (0,)), ((), ())), preferred_element_type=F32)
+
+
+def dot_nt(x, y):
+    return lax.dot_general(x, y, (((1,), (1,)), ((), ())), preferred_element_type=F32)
+
+
+def onehot(mask):
+    return jnp.where(mask, 1.0, 0.0).astype(BF16)
+
+
+def iotas(rows, cols):
+    return (lax.broadcasted_iota(jnp.int32, (rows, cols), 0),
+            lax.broadcasted_iota(jnp.int32, (rows, cols), 1))
+
+
 def physics(
-    start_ref, adj_ref, par_ref, wave_ref, src_ref, rec_ref, obs_ref, grad_ref,
+    model_ref, accum_ref, own_ref, aper_ref,
+    start_ref, adj_ref, wave_ref, src_ref, rec_ref, obs_ref, new_model_ref, new_accum_ref,
     F, C, W, A, B, DV, ST, CNT, OB, R0,
     send_l, send_r, recv_l, recv_r, ss_l, ss_r, rs_l, rs_r,
+    par_ref, grad_ref, GT, Y, OUT, RECV, RET, PSW, RETS, ARR, TP, TW, TH, SB, TF,
+    g_send, g_recv, p_send, p_recv, b_send, b_recv, x_send, x_recv, w_send, w_recv,
 ):
     n_sub = lax.axis_size("sub")
+    n_shot = lax.axis_size("shot")
     me = lax.axis_index("sub")
+    shot = lax.axis_index("shot")
+    rep = lax.axis_index("rep")
+    partner = {"rep": 1 - rep}
     has_l = me > 0
     has_r = me < n_sub - 1
     left = {"sub": jnp.maximum(me - 1, 0)}
     right = {"sub": jnp.minimum(me + 1, n_sub - 1)}
     barrier = pltpu.get_barrier_semaphore()
-
-    @pl.when(has_l)
-    def _():
-        pl.semaphore_signal(barrier, inc=1, device_id=left, device_id_type=MESH)
-
-    @pl.when(has_r)
-    def _():
-        pl.semaphore_signal(barrier, inc=1, device_id=right, device_id_type=MESH)
-
-    @pl.when(has_l)
-    def _():
-        pl.semaphore_wait(barrier, 1)
-
-    @pl.when(has_r)
-    def _():
-        pl.semaphore_wait(barrier, 1)
+    others = [{"shot": lax.rem(shot + j, n_shot)} for j in range(1, n_shot)]
+    others += [{"sub": lax.rem(me + j, n_sub)} for j in range(1, n_sub)]
+    others += [partner]
+    for other in others:
+        pl.semaphore_signal(barrier, inc=1, device_id=other, device_id_type=MESH)
+
+    n_slots = n_shot * TILES
+    n_pos = n_shot * SLAB_TILES
+    l8, l16 = max(LANES, n_shot * HALF), max(LANES, n_shot * 2 * HALF)
+    r_, c_ = iotas(n_slots, own_ref.shape[1])
+    perm = onehot(own_ref[...] == r_)
+    r_, c_ = iotas(own_ref.shape[1], n_pos)
+    named = onehot(aper_ref[...] == r_)
+    at = dot(perm, named).astype(BF16)
+    r_, c_ = iotas(n_slots, n_slots)
+    lower = onehot((r_ // TILES == c_ // TILES) & (c_ < r_))
+    r_, c_ = iotas(n_pos, l8)
+    occ = dot(at, onehot(r_ // SLAB_TILES == c_ // HALF))
+    rank = dot(lower, occ.astype(BF16))
+    r_, c_ = iotas(n_slots, l8)
+    place = (rep * HALF + c_ % HALF).astype(F32)
+    GT[...] = jnp.where(rank == place, occ, 0.0)
+    gt = GT[pl.ds(pl.multiple_of(shot * TILES, TILES), TILES)]
+    g = gt.T[: n_shot * HALF].astype(BF16)
+    gt = gt[:, : n_shot * HALF].astype(BF16)
+    columns = []
+    for b in range(TILE_Y):
+        for k in range(3):
+            columns.append(jnp.concatenate(
+                [model_ref[k, :, pl.ds((a * TILE_Y + b) * DEPTH, DEPTH)] for a in range(TILE_X)],
+                axis=1))
+    flat = jnp.concatenate(columns, axis=1)
+    outgoing = dot(jnp.concatenate([g, g, g], axis=1), jnp.concatenate(split3(flat), axis=0))
+    for b in range(TILE_Y):
+        OUT[:, b] = outgoing[:, b * QAC:(b + 1) * QAC].reshape(n_shot, HALF, QAC)
+
+    pl.semaphore_wait(barrier, len(others))
+
+    def gather(j):
+        return pltpu.make_async_remote_copy(
+            src_ref=OUT.at[lax.rem(shot + j, n_shot)], dst_ref=RECV.at[rep, shot],
+            send_sem=g_send.at[j], recv_sem=g_recv.at[j],
+            device_id={"shot": lax.rem(shot + j, n_shot)}, device_id_type=MESH)
+
+    def gather_in(j):
+        came = RECV.at[rep, lax.rem(shot + n_shot - j, n_shot)]
+        return pltpu.make_async_remote_copy(
+            src_ref=came, dst_ref=came, send_sem=g_send.at[j], recv_sem=g_recv.at[j],
+            device_id={"shot": lax.rem(shot + j, n_shot)}, device_id_type=MESH)
+
+    def share(j, half):
+        came = RECV.at[half, lax.rem(shot + n_shot - j, n_shot)]
+        return pltpu.make_async_remote_copy(
+            src_ref=came, dst_ref=came, send_sem=p_send.at[j], recv_sem=p_recv.at[j],
+            device_id=partner, device_id_type=MESH)
+
+    for j in range(n_shot - 1, 0, -1):
+        gather(j).start()
+    RECV[rep, shot] = OUT[shot]
+    share(0, rep).start()
 
     def copies(e):
         nl, nr = TO_PRIOR[e], TO_NEXT[e]
@@ -169,6 +247,8 @@
             F[i, x, :, pl.ds(0, WY)] = start_ref[i, x - 1].astype(F32)
             C[i, x - 1] = zero
             C[i, x - 1, :, pl.ds(0, WY)] = adj_ref[i, x - 1].astype(F32)
+
+    def with_model(x):
         B[x - 1] = jnp.where(inside, 1.0 / jnp.where(inside, par_ref[2, x - 1], 1.0), 0.0)
         strain_cot(x, [C[3 + i, x - 1] for i in range(6)])
 
@@ -178,8 +258,7 @@
     e3 = ([(F, 1), (F, 2), (A, 1), (A, 2)], [(F, 0), (A, 0)])
     e4 = ([(W, 0)], [(W, 3), (W, 4)])
 
-    edges_first(load, lambda: send(0, *e0))
-
+    lax.fori_loop(1, LX + 1, lambda x, _: (load(x), 0)[1], 0)
     cell = rec_ref[...]
     q = cell >> 5
     rx = (q * 52429) >> 22
@@ -200,6 +279,46 @@
     CNT[...] = spread(jnp.ones((1, nrec), F32)).reshape(LX, DEPTH, LANES)
     OB[0] = spread(obs_ref[0:1]).reshape(LX, DEPTH, LANES)
     OB[1] = spread(obs_ref[1:2]).reshape(LX, DEPTH, LANES)
+
+    r_, c_ = iotas(n_pos, l16)
+    occ = dot(at, onehot(r_ // SLAB_TILES == shot))
+    rank = dot(lower, occ.astype(BF16))
+    r_, c_ = iotas(n_slots, l16)
+    half_of = c_ // (n_shot * HALF)
+    owner_of = c_ // HALF - half_of * n_shot
+    place = (half_of * HALF + c_ % HALF).astype(F32)
+    chunk = jnp.where((rank == place) & (owner_of == r_ // TILES), occ, 0.0)
+    r_, c_ = iotas(n_pos, SLAB_XT * LANES)
+    pos = r_ % SLAB_TILES
+    in_y = c_ % LANES
+    cover = (r_ // SLAB_TILES == shot) & (pos // SLAB_YT == c_ // LANES)
+    cover = cover & (pos % SLAB_YT == in_y // TILE_Y)
+    cells_of = dot(at, onehot(cover)).astype(BF16)
+    where_ = dot(chunk.T.astype(BF16), cells_of)[: 2 * n_shot * HALF]
+    r_, c_ = iotas(2 * n_shot * HALF, SLAB_XT * LANES)
+    for b in range(TILE_Y):
+        part = jnp.where(c_ % LANES % TILE_Y == b, where_, 0.0)
+        Y[:, b] = part.reshape(2 * n_shot, HALF, SLAB_XT * LANES)
+    k_rows = 2 * n_shot * TILE_Y * HALF
+    ymat = Y[...].reshape(k_rows, SLAB_XT * LANES).astype(BF16)
+
+    for j in range(1, n_shot):
+        gather_in(j).wait_recv()
+        share(j, rep).start()
+    for j in range(n_shot):
+        share(j, 1 - rep).wait_recv()
+    came = RECV[...].reshape(k_rows, QAC).T
+    slab = None
+    for piece in split3(came):
+        term = dot(piece, ymat)
+        slab = term if slab is None else slab + term
+    for k in range(3):
+        for a in range(TILE_X):
+            for i in range(SLAB_XT):
+                par_ref[k, i * TILE_X + a] = slab[
+                    (k * TILE_X + a) * DEPTH:(k * TILE_X + a + 1) * DEPTH,
+                    i * LANES:(i + 1) * LANES]
+    edges_first(with_model, lambda: send(0, *e0))
 
     scell = src_ref[0]
     sq = scell >> 5
@@ -321,107 +440,163 @@
     lax.fori_loop(1, LX + 1, lambda x, _: (last_velocity(x), 0)[1], 0)
 
 
-def run_physics(start, adj, params, wave, src, rec, obs):
+    rows_ = []
+    for k in range(3):
+        for a in range(TILE_X):
+            rows_.append(jnp.concatenate(
+                [grad_ref[k, i * TILE_X + a] for i in range(SLAB_XT)], axis=1))
+    rows_ = jnp.concatenate(rows_, axis=0)
+    back = None
+    for piece in split3(rows_):
+        term = dot_nt(ymat, piece)
+        back = term if back is None else back + term
+    RET[...] = back.reshape(2, n_shot, TILE_Y, HALF, QAC)
+
+    def swap(src, dst, k):
+        return pltpu.make_async_remote_copy(
+            src_ref=src, dst_ref=dst, send_sem=w_send.at[k], recv_sem=w_recv.at[k],
+            device_id=partner, device_id_type=MESH)
+
+    for j in range(n_shot):
+        o = lax.rem(shot + n_shot - j, n_shot)
+        swap(RET.at[1 - rep, o], PSW.at[o], j).start()
+
+    def give(j):
+        return pltpu.make_async_remote_copy(
+            src_ref=RETS.at[lax.rem(shot + n_shot - j, n_shot)], dst_ref=ARR.at[shot],
+            send_sem=b_send.at[j], recv_sem=b_recv.at[j],
+            device_id={"shot": lax.rem(shot + n_shot - j, n_shot)}, device_id_type=MESH)
+
+    def give_in(j):
+        o = lax.rem(shot + j, n_shot)
+        return pltpu.make_async_remote_copy(
+            src_ref=ARR.at[o], dst_ref=ARR.at[o], send_sem=b_send.at[j],
+            recv_sem=b_recv.at[j], device_id={"shot": o}, device_id_type=MESH)
+
+    for j in list(range(1, n_shot)) + [0]:
+        o = lax.rem(shot + n_shot - j, n_shot)
+        swap(RET.at[1 - rep, o], PSW.at[o], j).wait_recv()
+        if j > 0:
+            RETS[o] = RET[rep, o] + PSW[o]
+            give(j).start()
+        else:
+            ARR[o] = RET[rep, o] + PSW[o]
+    for j in range(1, n_shot):
+        give_in(j).wait_recv()
+    ggg = jnp.concatenate([gt, gt, gt], axis=1)
+    half_rows = TILES // 2
+    for b in range(TILE_Y):
+        arrived = ARR[:, b].reshape(n_shot * HALF, QAC)
+        part = dot(ggg, jnp.concatenate(split3(arrived), axis=0))
+        TP[0, b] = part[:half_rows]
+        TP[1, b] = part[half_rows:]
+
+    first = swap(TP.at[1 - rep], TW, n_shot)
+    first.start()
+    first.wait()
+    SB[me] = TP[rep] + TW[...]
+
+    def across(j):
+        return pltpu.make_async_remote_copy(
+            src_ref=SB.at[me], dst_ref=SB.at[me], send_sem=x_send.at[j], recv_sem=x_recv.at[j],
+            device_id={"sub": lax.rem(me + j, n_sub)}, device_id_type=MESH)
+
+    def across_in(j):
+        u = lax.rem(me + n_sub - j, n_sub)
+        return pltpu.make_async_remote_copy(
+            src_ref=SB.at[u], dst_ref=SB.at[u], send_sem=x_send.at[j], recv_sem=x_recv.at[j],
+            device_id={"sub": lax.rem(me + j, n_sub)}, device_id_type=MESH)
+
+    for j in range(1, n_sub):
+        across(j).start()
+    for j in range(1, n_sub):
+        across_in(j).wait_recv()
+    total = SB[0]
+    for u in range(1, n_sub):
+        total = total + SB[u]
+    TF[rep] = total
+    TH[...] = total
+    last = swap(TH, TF.at[rep], n_shot + 1)
+    last.start()
+    pltpu.make_async_remote_copy(
+        src_ref=TH, dst_ref=TF.at[1 - rep], send_sem=w_send.at[n_shot + 1],
+        recv_sem=w_recv.at[n_shot + 1], device_id=partner, device_id_type=MESH).wait_recv()
+
+    for k in range(3):
+        for h in range(2):
+            grad = jnp.concatenate(
+                [TF[h, b, :, pl.ds((k * TILE_X + a) * DEPTH, DEPTH)]
+                 for a in range(TILE_X) for b in range(TILE_Y)], axis=1)
+            rows = pl.ds(h * half_rows, half_rows)
+            new_accum = accum_ref[k, rows] + grad * grad
+            new_accum_ref[k, rows] = new_accum
+            new_model_ref[k, rows] = model_ref[k, rows] - learn_rate * grad / jnp.sqrt(new_accum)
+
+    last.wait_send()
+    for j in range(1, n_shot):
+        gather(j).wait_send()
+        give(j).wait_send()
+    for j in range(n_shot):
+        o = lax.rem(shot + n_shot - j, n_shot)
+        share(j, rep).wait_send()
+        swap(RET.at[1 - rep, o], PSW.at[o], j).wait_send()
+    for j in range(1, n_sub):
+        across(j).wait_send()
+
+
+def run_window(model, accum, own, aper, start, adj, wave, src, rec, obs):
+    n_shot = lax.axis_size("shot")
+    n_sub = lax.axis_size("sub")
     vm = pl.BlockSpec(memory_space=pltpu.VMEM)
     sm = pl.BlockSpec(memory_space=pltpu.SMEM)
     layer = (DEPTH, LANES)
+    half = TILES // 2
+    dma = pltpu.SemaphoreType.DMA
     halo = pltpu.VMEM((5, 4) + layer, F32)
-    dma = pltpu.SemaphoreType.DMA((5,))
+    rim = dma((5,))
+
+    def vmem(*shape):
+        return pltpu.VMEM(shape, F32)
+
+    chunk = (TILE_Y, HALF, QAC)
     return pl.pallas_call(
         physics,
-        out_shape=jax.ShapeDtypeStruct((3, LX) + layer, F32),
-        in_specs=[vm, vm, vm, sm, sm, vm, vm],
-        out_specs=vm,
+        out_shape=[jax.ShapeDtypeStruct(model.shape, F32)] * 2,
+        in_specs=[vm, vm, vm, vm, vm, vm, sm, sm, vm, vm],
+        out_specs=[vm, vm],
         scratch_shapes=[
-            pltpu.VMEM((9, LX + 2) + layer, F32),
-            pltpu.VMEM((9, LX) + layer, F32),
-            pltpu.VMEM((6, LX + 2) + layer, F32),
-            pltpu.VMEM((3, LX + 2) + layer, F32),
-            pltpu.VMEM((LX,) + layer, F32),
-            pltpu.VMEM((3, LX) + layer, F32),
-            pltpu.VMEM((6, LX) + layer, F32),
-            pltpu.VMEM((LX,) + layer, F32),
-            pltpu.VMEM((2, LX) + layer, F32),
-            pltpu.VMEM((LX,) + layer, F32),
-            halo, halo, halo, halo, dma, dma, dma, dma,
+            vmem(9, LX + 2, *layer), vmem(9, LX, *layer), vmem(6, LX + 2, *layer),
+            vmem(3, LX + 2, *layer), vmem(LX, *layer), vmem(3, LX, *layer),
+            vmem(6, LX, *layer), vmem(LX, *layer), vmem(2, LX, *layer), vmem(LX, *layer),
+            halo, halo, halo, halo, rim, rim, rim, rim,
+            vmem(3, LX, *layer), vmem(3, LX, *layer),
+            vmem(n_shot * TILES, max(LANES, n_shot * HALF)),
+            vmem(2 * n_shot, TILE_Y, HALF, SLAB_XT * LANES),
+            vmem(n_shot, *chunk), vmem(2, n_shot, *chunk), vmem(2, n_shot, *chunk),
+            vmem(n_shot, *chunk), vmem(n_shot, *chunk), vmem(n_shot, *chunk),
+            vmem(2, TILE_Y, half, QAC), vmem(TILE_Y, half, QAC), vmem(TILE_Y, half, QAC),
+            vmem(n_sub, TILE_Y, half, QAC), vmem(2, TILE_Y, half, QAC),
+            dma((n_shot,)), dma((n_shot,)), dma((n_shot,)), dma((n_shot,)),
+            dma((n_shot,)), dma((n_shot,)), dma((n_sub,)), dma((n_sub,)),
+            dma((n_shot + 2,)), dma((n_shot + 2,)),
         ],
         compiler_params=pltpu.CompilerParams(
-            collective_id=0, has_side_effects=True, vmem_limit_bytes=40 * 1024 * 1024),
-    )(start, adj, params, wave, src, rec, obs)
+            collective_id=0, has_side_effects=True, vmem_limit_bytes=52 * 1024 * 1024),
+    )(model, accum, own, aper, start, adj, wave, src, rec, obs)
 
 
 def on_device(
-    model,
-    accum,
-    owner_map,
-    aperture,
-    start_state,
-    adjoint_end,
-    wavelet,
-    source_cell,
-    receiver_cell,
-    observed,
+    model, accum, owner_map, aperture, start_state, adjoint_end, wavelet, source_cell,
+    receiver_cell, observed,
 ):
-    n_shot = lax.axis_size("shot")
-    my_shot = lax.axis_index("shot")
-    tiles_dev = model.shape[0]
-    tile_cells = model.shape[2]
-    per_owner = 2 * SLAB_TILES // n_shot
-    slab_slots = owner_map[aperture[:, 0, :]]
-    owners = slab_slots // tiles_dev
-    local_rows = slab_slots % tiles_dev
-    positions = jnp.arange(SLAB_TILES, dtype=jnp.int32)
-    earlier = (owners[:, :, None] == owners[:, None, :]) & (
-        positions[None, None, :] < positions[None, :, None]
-    )
-    ranks = jnp.sum(earlier.astype(jnp.int32), axis=2)
-    slot_ids = jnp.arange(per_owner, dtype=jnp.int32)
-    serve = (owners[:, None, :] == my_shot) & (ranks[:, None, :] == slot_ids[None, :, None])
-    served = jnp.any(serve, axis=2)
-    serve_rows = jnp.sum(jnp.where(serve, local_rows[:, None, :], 0), axis=2)
-    outgoing = jnp.where(served[:, :, None, None], model[serve_rows], 0.0)
-    incoming = lax.all_to_all(outgoing, "shot", split_axis=0, concat_axis=0, tiled=True)
-    my_owners = owners[my_shot]
-    my_ranks = ranks[my_shot]
-    slab = incoming.reshape(n_shot * per_owner, 3, tile_cells)[my_owners * per_owner + my_ranks]
-    slab_x = SLAB_XT * TILE_X
-    slab_y = SLAB_YT * TILE_Y
-    params = slab.reshape(SLAB_XT, SLAB_YT, 3, TILE_X, TILE_Y, DEPTH)
-    params = params.transpose(2, 0, 3, 5, 1, 4).reshape(3, slab_x, DEPTH, slab_y)
-    params = jnp.pad(params, ((0, 0), (0, 0), (0, 0), (0, LANES - slab_y)))
     start = start_state[0, 0, 0].transpose(0, 1, 3, 2)
     adj = adjoint_end[0, 0, 0].transpose(0, 1, 3, 2)
-    gradient = run_physics(
-        start, adj, params, wavelet.reshape(NSTEPS), source_cell.reshape(1),
+    new_model, new_accum = run_window(
+        model.transpose(1, 0, 2), accum.transpose(1, 0, 2), owner_map.reshape(1, -1),
+        aperture.reshape(1, -1), start, adj, wavelet.reshape(NSTEPS), source_cell.reshape(1),
         receiver_cell.reshape(1, -1), observed[0, 0, 0],
-    )[..., :slab_y]
-    back = gradient.reshape(3, SLAB_XT, TILE_X, DEPTH, SLAB_YT, TILE_Y)
-    back = back.transpose(1, 4, 0, 2, 5, 3).reshape(SLAB_TILES, 3, tile_cells)
-    all_slots = jnp.arange(per_owner, dtype=jnp.int32)
-    owner_ids = jnp.arange(n_shot, dtype=jnp.int32)
-    place = (my_owners[None, None, :] == owner_ids[:, None, None]) & (
-        my_ranks[None, None, :] == all_slots[None, :, None]
     )
-    placed = jnp.any(place, axis=2)
-    place_rows = jnp.sum(jnp.where(place, positions[None, None, :], 0), axis=2)
-    returning = jnp.where(placed[:, :, None, None], back[place_rows], 0.0)
-    arrived = lax.all_to_all(returning, "shot", split_axis=0, concat_axis=0, tiled=True)
-    pick = (
-        serve_rows[:, :, None] == jnp.arange(tiles_dev, dtype=jnp.int32)[None, None, :]
-    ) & served[:, :, None]
-    pick = pick.astype(jnp.float32).reshape(n_shot * per_owner, tiles_dev)
-    partial_sum = jnp.einsum(
-        "sd,sc->dc",
-        pick,
-        arrived.reshape(n_shot * per_owner, 3 * tile_cells),
-        precision=lax.Precision.HIGHEST,
-        preferred_element_type=jnp.float32,
-    )
-    partial_sum = partial_sum.reshape(tiles_dev, 3, tile_cells)
-    total = lax.psum(partial_sum, ("sub", "rep"))
-    new_accum = accum + total * total
-    new_model = model - learn_rate * total / jnp.sqrt(new_accum)
-    return (new_model, new_accum)
+    return (new_model.transpose(1, 0, 2), new_accum.transpose(1, 0, 2))
 
 
 def solution(mesh):

time: 111 us -> 54.3 us (0.49); the launches traced: 109 us -> 53.9 us
  waiting for transfers between devices: 57.2 us -> 0 us
  Pallas kernels: 13.6 us -> 46.2 us
  between operations: 14.9 us -> 1.32 us
  starting transfers between devices: 9.06 us -> 0 us
  other arithmetic: 5.28 us -> 0.69 us
  local copies, waits for them, and re-layouts: 8.26 us -> 5.69 us
    psum x1 -> x0, waiting for transfers between devices: 36.3 us -> none  [on_device(): total = lax.psum(partial_sum, ('sub', 'rep'))]
    pallas_call x1, Pallas kernels: 13.6 us -> 46.2 us  [run_window(): pl.pallas_call(physics, out_shape=[jax.ShapeDtypeStruct(model.shape, F32)...]
    all_to_all x2 -> x0, waiting for transfers between devices: 20.8 us -> none  [the longest x1 12.2 us: on_device(): lax.all_to_all(outgoing, 'shot', split_axis=0, concat_axis=0, tiled=True)]
    all_to_all x2 -> x0, starting transfers between devices: 9.02 us -> none  [the longest x1 5.42 us: on_device(): lax.all_to_all(outgoing, 'shot', split_axis=0, concat_axis=0, tiled=True)]
    unnamed x16 -> x19, local copies, waits for them, and re-layouts: 0.87 us -> 5.6 us
    gather x6 -> x0, local copies, waits for them, and re-layouts: 4.36 us -> none  [the longest x1 1.31 us: on_device(): outgoing = jnp.where(served[:, :, None, None], model[serve_rows], 0.0)]
    select_n x7 -> x0, other arithmetic: 2.53 us -> none  [the longest x2 0.88 us: on_device(): returning = jnp.where(placed[:, :, None, None], back[place_rows], 0.0)]
    sub x1 -> x0, other arithmetic: 1.78 us -> none  [on_device(): new_model = model - learn_rate * total / jnp.sqrt(new_accum)]
  transfers between devices with their start and end apart: 3 -> 0, of which waited for: 3 -> 0; matrix products, arithmetic and copies ran while one was open for 0% -> 0% of each run, Pallas kernels for 0% -> 0%
where the time goes in v2:
time: 54.3 us; the launch traced here: 53.9 us
  Pallas kernels  46.2 us (85%)
  local copies, waits for them, and re-layouts  5.69 us (10%)
  between operations  1.32 us (2%)
  other arithmetic  0.69 us (1%)
    pallas_call x1, Pallas kernels, run_window(): pl.pallas_call(physics, out_shape=[jax.ShapeDtypeStruct(model.shape, F32)...  46.2 us
    unnamed x19, local copies, waits for them, and re-layouts  5.6 us

profile of v2, /device:TPU:1, one launch (start us, length us, event | category | flops | bytes accessed | tf_op | source)
XLA Modules:
  0.0 53.9 jit_solution(12094656467103112932)
XLA Ops:
  1.3 0.0 copy-start.7
  1.3 0.5 broadcast.3
  1.8 0.2 copy-done.7
  2.0 0.0 copy-start.4
  2.0 0.0 copy-start.6
  2.0 0.7 %reduce.3 = s32[4,32]{1,0:T(4,128)S(1)} reduce(s32[4,1,32]{2,1,0:T(1,128)S(1)} %copy-done.7, s32[]{:T(128)} %broadcast.3), dimensions={1}, to_apply=%param.13.reduce_sub_computation.3 | reduce | bytes 1028 | tf_op args[3]
  2.7 0.0 copy-start.3
  2.7 0.0 copy-start.5
  2.7 0.1 reshape.20.aper_ref
  2.8 0.0 copy-done.4
  2.8 0.0 copy-done.6
  2.8 0.6 %copy-done.3 = f32[1,1,1,2,256]{4,3,2,1,0:T(2,128)S(1)} copy-done((f32[1,1,1,2,256]{4,3,2,1,0:T(2,128)S(1)}, f32[1,1,1,2,256]{4,3,2,1,0:T(2,128)}, u32[]{:S(2)}) %copy-start.3) | copy-done | bytes 2072
  3.3 0.0 copy-done.5
  3.3 0.0 copy-start
  3.3 1.1 %copy-done = bf16[1,1,1,9,8,80,32]{5,6,4,3,2,1,0:T(8,128)(2,1)S(1)} copy-done((bf16[1,1,1,9,8,80,32]{5,6,4,3,2,1,0:T(8,128)(2,1)S(1)}, bf16[1,1,1,9,8,80,32]{5,6,4,3,2,1,0:T(8,128)(2,1)}, u32[]{:S(2)}) %copy-start) | copy-done | bytes 368664
  4.4 0.0 copy-start.1
  4.4 0.9 %copy-done.1 = f32[32,3,640]{2,0,1:T(8,128)S(1)} copy-done((f32[32,3,640]{2,0,1:T(8,128)S(1)}, f32[32,3,640]{2,0,1:T(8,128)}, u32[]{:S(2)}) %copy-start.1) | copy-done | bytes 245784
  5.4 0.0 copy-start.2
  5.4 0.9 %copy-done.2 = f32[32,3,640]{2,0,1:T(8,128)S(1)} copy-done((f32[32,3,640]{2,0,1:T(8,128)S(1)}, f32[32,3,640]{2,0,1:T(8,128)}, u32[]{:S(2)}) %copy-start.2) | copy-done | bytes 245784
  6.3 46.2 %shard_map.113 = (f32[3,32,640]{2,1,0:T(8,128)S(1)}, f32[3,32,640]{2,1,0:T(8,128)S(1)}) custom-call(f32[3,32,640]{2,1,0:T(8,128)S(1)} %bitcast.17, f32[3,32,640]{2,1,0:T(8,128)S(1)} %bitcast.18, s32[1,128]{1,0:T(1,128)S(1)} %bitcast.23, s32[1,128]{1,0:T(1,128)S(1)} %reshape.20.aper_ref, bf16[9,8,32,80]{3,2,1,0:T(8,128)(2,1)S(1)} %bitcast.16, ...), custom_call_target="tpu_custom_call" | custom-call | tf_op jit(solution)/shard_map/pallas_call | solution.py:562
  52.6 0.7 %copy.15 = f32[32,3,640]{2,0,1:T(8,128)} copy(f32[32,3,640]{2,0,1:T(8,128)S(1)} %bitcast.20) | data formatting | bytes 491520
  53.2 0.7 %copy.16 = f32[32,3,640]{2,0,1:T(8,128)} copy(f32[32,3,640]{2,0,1:T(8,128)S(1)} %bitcast.19) | data formatting | bytes 491520
Async XLA Ops:
  1.3 0.7 %copy-start.7 = (s32[4,1,32]{2,1,0:T(1,128)S(1)}, s32[4,1,32]{2,1,0:T(1,128)}, u32[]{:S(2)}) copy-start(s32[4,1,32]{2,1,0:T(1,128)} %param.13) | copy-start | bytes 1540
  2.0 0.8 %copy-start.4 = (s32[1,1,1,256]{3,2,1,0:T(1,128)S(1)}, s32[1,1,1,256]{3,2,1,0:T(1,128)}, u32[]{:S(2)}) copy-start(s32[1,1,1,256]{3,2,1,0:T(1,128)} %param.18) | copy-start | bytes 3076
  2.0 0.8 %copy-start.6 = (f32[1,1,1,2]{3,2,1,0:T(1,128)S(1)}, f32[1,1,1,2]{3,2,1,0:T(1,128)}, u32[]{:S(2)}) copy-start(f32[1,1,1,2]{3,2,1,0:T(1,128)} %param.16) | copy-start | bytes 28
  2.7 0.7 %copy-start.3 = (f32[1,1,1,2,256]{4,3,2,1,0:T(2,128)S(1)}, f32[1,1,1,2,256]{4,3,2,1,0:T(2,128)}, u32[]{:S(2)}) copy-start(f32[1,1,1,2,256]{4,3,2,1,0:T(2,128)} %param.19) | copy-start | bytes 6148
  2.7 0.7 %copy-start.5 = (s32[128]{0:T(128)S(1)}, s32[128]{0:T(128)}, u32[]{:S(2)}) copy-start(s32[128]{0:T(128)} %param.12) | copy-start | bytes 1540
  3.3 1.1 %copy-start = (bf16[1,1,1,9,8,80,32]{5,6,4,3,2,1,0:T(8,128)(2,1)S(1)}, bf16[1,1,1,9,8,80,32]{5,6,4,3,2,1,0:T(8,128)(2,1)}, u32[]{:S(2)}) copy-start(bf16[1,1,1,9,8,80,32]{5,6,4,3,2,1,0:T(8,128)(2,1)} %param.14) | copy-start | bytes 1105924
  4.4 0.9 %copy-start.1 = (f32[32,3,640]{2,0,1:T(8,128)S(1)}, f32[32,3,640]{2,0,1:T(8,128)}, u32[]{:S(2)}) copy-start(f32[32,3,640]{2,0,1:T(8,128)} %param.10) | copy-start | bytes 737284
  5.4 0.9 %copy-start.2 = (f32[32,3,640]{2,0,1:T(8,128)S(1)}, f32[32,3,640]{2,0,1:T(8,128)}, u32[]{:S(2)}) copy-start(f32[32,3,640]{2,0,1:T(8,128)} %param.11) | copy-start | bytes 737284

commit v3 on v2

--- a/solution.py
+++ b/solution.py
@@ -62,13 +62,22 @@
 
 
 def physics(
-    model_ref, accum_ref, own_ref, aper_ref,
-    start_ref, adj_ref, wave_ref, src_ref, rec_ref, obs_ref, new_model_ref, new_accum_ref,
+    model_hbm, accum_hbm, own_ref, aper_ref,
+    start_hbm, adj_hbm, wave_ref, src_ref, rec_ref, obs_ref, new_model_ref, new_accum_ref,
     F, C, W, A, B, DV, ST, CNT, OB, R0,
     send_l, send_r, recv_l, recv_r, ss_l, ss_r, rs_l, rs_r,
     par_ref, grad_ref, GT, Y, OUT, RECV, RET, PSW, RETS, ARR, TP, TW, TH, SB, TF,
     g_send, g_recv, p_send, p_recv, b_send, b_recv, x_send, x_recv, w_send, w_recv,
+    model_ref, accum_ref, start_ref, adj_ref, l_sem, v_send, v_recv, y_send, y_recv,
 ):
+    fetch = [
+        pltpu.make_async_copy(src, dst, l_sem.at[i])
+        for i, (src, dst) in enumerate([
+            (model_hbm, model_ref), (start_hbm, start_ref), (adj_hbm, adj_ref),
+            (accum_hbm, accum_ref)])
+    ]
+    for copy in fetch:
+        copy.start()
     n_sub = lax.axis_size("sub")
     n_shot = lax.axis_size("shot")
     me = lax.axis_index("sub")
@@ -92,7 +101,8 @@
     r_, c_ = iotas(n_slots, own_ref.shape[1])
     perm = onehot(own_ref[...] == r_)
     r_, c_ = iotas(own_ref.shape[1], n_pos)
-    named = onehot(aper_ref[...] == r_)
+    ids = jnp.concatenate([aper_ref[s] for s in range(n_shot)], axis=1)
+    named = onehot(ids == r_)
     at = dot(perm, named).astype(BF16)
     r_, c_ = iotas(n_slots, n_slots)
     lower = onehot((r_ // TILES == c_ // TILES) & (c_ < r_))
@@ -105,6 +115,7 @@
     gt = GT[pl.ds(pl.multiple_of(shot * TILES, TILES), TILES)]
     g = gt.T[: n_shot * HALF].astype(BF16)
     gt = gt[:, : n_shot * HALF].astype(BF16)
+    fetch[0].wait()
     columns = []
     for b in range(TILE_Y):
         for k in range(3):
@@ -258,6 +269,8 @@
     e3 = ([(F, 1), (F, 2), (A, 1), (A, 2)], [(F, 0), (A, 0)])
     e4 = ([(W, 0)], [(W, 3), (W, 4)])
 
+    fetch[1].wait()
+    fetch[2].wait()
     lax.fori_loop(1, LX + 1, lambda x, _: (load(x), 0)[1], 0)
     cell = rec_ref[...]
     q = cell >> 5
@@ -485,42 +498,53 @@
         give_in(j).wait_recv()
     ggg = jnp.concatenate([gt, gt, gt], axis=1)
     half_rows = TILES // 2
+
+    def to_core(b):
+        return pltpu.make_async_remote_copy(
+            src_ref=TP.at[1 - rep, b], dst_ref=TW.at[b], send_sem=v_send.at[b],
+            recv_sem=v_recv.at[b], device_id=partner, device_id_type=MESH)
+
+    def across(j, b):
+        return pltpu.make_async_remote_copy(
+            src_ref=SB.at[me, b], dst_ref=SB.at[me, b], send_sem=x_send.at[j, b],
+            recv_sem=x_recv.at[j, b], device_id={"sub": lax.rem(me + j, n_sub)},
+            device_id_type=MESH)
+
+    def across_in(j, b):
+        u = lax.rem(me + n_sub - j, n_sub)
+        return pltpu.make_async_remote_copy(
+            src_ref=SB.at[u, b], dst_ref=SB.at[u, b], send_sem=x_send.at[j, b],
+            recv_sem=x_recv.at[j, b], device_id={"sub": lax.rem(me + j, n_sub)},
+            device_id_type=MESH)
+
+    def last(b, half):
+        return pltpu.make_async_remote_copy(
+            src_ref=TH.at[b], dst_ref=TF.at[half, b], send_sem=y_send.at[b],
+            recv_sem=y_recv.at[b], device_id=partner, device_id_type=MESH)
+
     for b in range(TILE_Y):
         arrived = ARR[:, b].reshape(n_shot * HALF, QAC)
         part = dot(ggg, jnp.concatenate(split3(arrived), axis=0))
         TP[0, b] = part[:half_rows]
         TP[1, b] = part[half_rows:]
-
-    first = swap(TP.at[1 - rep], TW, n_shot)
-    first.start()
-    first.wait()
-    SB[me] = TP[rep] + TW[...]
-
-    def across(j):
-        return pltpu.make_async_remote_copy(
-            src_ref=SB.at[me], dst_ref=SB.at[me], send_sem=x_send.at[j], recv_sem=x_recv.at[j],
-            device_id={"sub": lax.rem(me + j, n_sub)}, device_id_type=MESH)
-
-    def across_in(j):
-        u = lax.rem(me + n_sub - j, n_sub)
-        return pltpu.make_async_remote_copy(
-            src_ref=SB.at[u], dst_ref=SB.at[u], send_sem=x_send.at[j], recv_sem=x_recv.at[j],
-            device_id={"sub": lax.rem(me + j, n_sub)}, device_id_type=MESH)
-
-    for j in range(1, n_sub):
-        across(j).start()
-    for j in range(1, n_sub):
-        across_in(j).wait_recv()
-    total = SB[0]
-    for u in range(1, n_sub):
-        total = total + SB[u]
-    TF[rep] = total
-    TH[...] = total
-    last = swap(TH, TF.at[rep], n_shot + 1)
-    last.start()
-    pltpu.make_async_remote_copy(
-        src_ref=TH, dst_ref=TF.at[1 - rep], send_sem=w_send.at[n_shot + 1],
-        recv_sem=w_recv.at[n_shot + 1], device_id=partner, device_id_type=MESH).wait_recv()
+        to_core(b).start()
+    for b in range(TILE_Y):
+        to_core(b).wait_recv()
+        SB[me, b] = TP[rep, b] + TW[b]
+        for j in range(1, n_sub):
+            across(j, b).start()
+    for b in range(TILE_Y):
+        for j in range(1, n_sub):
+            across_in(j, b).wait_recv()
+        total = SB[0, b]
+        for u in range(1, n_sub):
+            total = total + SB[u, b]
+        TF[rep, b] = total
+        TH[b] = total
+        last(b, rep).start()
+    fetch[3].wait()
+    for b in range(TILE_Y):
+        last(b, 1 - rep).wait_recv()
 
     for k in range(3):
         for h in range(2):
@@ -532,7 +556,11 @@
             new_accum_ref[k, rows] = new_accum
             new_model_ref[k, rows] = model_ref[k, rows] - learn_rate * grad / jnp.sqrt(new_accum)
 
-    last.wait_send()
+    for b in range(TILE_Y):
+        last(b, rep).wait_send()
+        to_core(b).wait_send()
+        for j in range(1, n_sub):
+            across(j, b).wait_send()
     for j in range(1, n_shot):
         gather(j).wait_send()
         give(j).wait_send()
@@ -540,8 +568,6 @@
         o = lax.rem(shot + n_shot - j, n_shot)
         share(j, rep).wait_send()
         swap(RET.at[1 - rep, o], PSW.at[o], j).wait_send()
-    for j in range(1, n_sub):
-        across(j).wait_send()
 
 
 def run_window(model, accum, own, aper, start, adj, wave, src, rec, obs):
@@ -549,6 +575,7 @@
     n_sub = lax.axis_size("sub")
     vm = pl.BlockSpec(memory_space=pltpu.VMEM)
     sm = pl.BlockSpec(memory_space=pltpu.SMEM)
+    hbm = pl.BlockSpec(memory_space=pltpu.HBM)
     layer = (DEPTH, LANES)
     half = TILES // 2
     dma = pltpu.SemaphoreType.DMA
@@ -562,7 +589,7 @@
     return pl.pallas_call(
         physics,
         out_shape=[jax.ShapeDtypeStruct(model.shape, F32)] * 2,
-        in_specs=[vm, vm, vm, vm, vm, vm, sm, sm, vm, vm],
+        in_specs=[hbm, hbm, vm, vm, hbm, hbm, sm, sm, vm, vm],
         out_specs=[vm, vm],
         scratch_shapes=[
             vmem(9, LX + 2, *layer), vmem(9, LX, *layer), vmem(6, LX + 2, *layer),
@@ -577,11 +604,14 @@
             vmem(2, TILE_Y, half, QAC), vmem(TILE_Y, half, QAC), vmem(TILE_Y, half, QAC),
             vmem(n_sub, TILE_Y, half, QAC), vmem(2, TILE_Y, half, QAC),
             dma((n_shot,)), dma((n_shot,)), dma((n_shot,)), dma((n_shot,)),
-            dma((n_shot,)), dma((n_shot,)), dma((n_sub,)), dma((n_sub,)),
-            dma((n_shot + 2,)), dma((n_shot + 2,)),
+            dma((n_shot,)), dma((n_shot,)), dma((n_sub, TILE_Y)), dma((n_sub, TILE_Y)),
+            dma((n_shot,)), dma((n_shot,)),
+            vmem(*model.shape), vmem(*accum.shape),
+            pltpu.VMEM(start.shape, start.dtype), pltpu.VMEM(adj.shape, adj.dtype),
+            dma((4,)), dma((TILE_Y,)), dma((TILE_Y,)), dma((TILE_Y,)), dma((TILE_Y,)),
         ],
         compiler_params=pltpu.CompilerParams(
-            collective_id=0, has_side_effects=True, vmem_limit_bytes=52 * 1024 * 1024),
+            collective_id=0, has_side_effects=True, vmem_limit_bytes=63 * 1024 * 1024),
     )(model, accum, own, aper, start, adj, wave, src, rec, obs)
 
 
@@ -593,7 +623,7 @@
     adj = adjoint_end[0, 0, 0].transpose(0, 1, 3, 2)
     new_model, new_accum = run_window(
         model.transpose(1, 0, 2), accum.transpose(1, 0, 2), owner_map.reshape(1, -1),
-        aperture.reshape(1, -1), start, adj, wavelet.reshape(NSTEPS), source_cell.reshape(1),
+        aperture, start, adj, wavelet.reshape(NSTEPS), source_cell.reshape(1),
         receiver_cell.reshape(1, -1), observed[0, 0, 0],
     )
     return (new_model.transpose(1, 0, 2), new_accum.transpose(1, 0, 2))

time: 54.3 us -> 50.6 us (0.932)
  local copies, waits for them, and re-layouts: 5.69 us -> 2.39 us
  other arithmetic: 0.69 us -> 0 us
    unnamed x19 -> x4, local copies, waits for them, and re-layouts: 5.6 us -> 2.39 us
    unnamed x1 -> x0, other arithmetic: 0.69 us -> none
where the time goes in v3:
time: 50.6 us; the launch traced here: 50.4 us
  Pallas kernels  46.7 us (92%)
  local copies, waits for them, and re-layouts  2.39 us (5%)
  between operations  1.3 us (3%)
    pallas_call x1, Pallas kernels, run_window(): pl.pallas_call(physics, out_shape=[jax.ShapeDtypeStruct(model.shape, F32)...  46.7 us
    unnamed x4, local copies, waits for them, and re-layouts  2.39 us

profile of v3, /device:TPU:1, one launch (start us, length us, event | category | flops | bytes accessed | tf_op | source)
XLA Modules:
  0.0 50.4 jit_solution(5929831883438660326)
XLA Ops:
  1.3 46.7 %shard_map.113 = (f32[3,32,640]{2,1,0:T(8,128)}, f32[3,32,640]{2,1,0:T(8,128)}) custom-call(f32[3,32,640]{2,1,0:T(8,128)} %bitcast.18, f32[3,32,640]{2,1,0:T(8,128)} %bitcast.19, s32[1,128]{1,0:T(1,128)} %bitcast.24, s32[4,1,32]{2,1,0:T(1,128)} %aper_ref.1, bf16[9,8,32,80]{3,2,1,0:T(8,128)(2,1)} %bitcast.16, bf16[9,8,32,80]{3,2,1,0:T(8,128)(2,1)} %bitcast.17, ...), custom_call_target="tpu_custom_call" | custom-call | tf_op jit(solution)/shard_map/pallas_call | solution.py:589
  48.0 0.0 copy-start
  48.0 1.7 %copy.15 = f32[32,3,640]{2,0,1:T(8,128)} copy(f32[32,3,640]{2,0,1:T(8,128)} %bitcast.21) | data formatting | bytes 491520
  49.7 0.0 copy-done
  49.7 0.7 %copy.16 = f32[32,3,640]{2,0,1:T(8,128)} copy(f32[32,3,640]{2,0,1:T(8,128)S(1)} %bitcast.20) | data formatting | bytes 491520
Async XLA Ops:
  48.0 1.7 %copy-start = (f32[3,32,640]{2,1,0:T(8,128)S(1)}, f32[3,32,640]{2,1,0:T(8,128)}, u32[]{:S(2)}) copy-start(f32[3,32,640]{2,1,0:T(8,128)} %get-tuple-element.5) | copy-start | bytes 737284

commit v4 on v3

--- a/solution.py
+++ b/solution.py
@@ -280,16 +280,18 @@
     nrec = rec_ref.shape[1]
     rows = lax.broadcasted_iota(jnp.int32, (LX * DEPTH, nrec), 0)
     cols = lax.broadcasted_iota(jnp.int32, (LANES, nrec), 0)
-    at_row = jnp.where(rows == rrow, 1.0, 0.0).astype(F32)
+    at_row = onehot(rows == rrow)
     at_col = cols == ry
-    dims = (((1,), (1,)), ((), ()))
 
     def spread(values):
-        return lax.dot_general(
-            at_row, jnp.where(at_col, values, 0.0), dims,
-            precision=lax.Precision.HIGHEST, preferred_element_type=F32)
-
-    CNT[...] = spread(jnp.ones((1, nrec), F32)).reshape(LX, DEPTH, LANES)
+        out = None
+        for piece in split3(values):
+            term = dot_nt(at_row, jnp.where(at_col, piece.astype(F32), 0.0).astype(BF16))
+            out = term if out is None else out + term
+        return out
+
+    count = dot_nt(at_row, onehot(at_col))
+    CNT[...] = count.reshape(LX, DEPTH, LANES)
     OB[0] = spread(obs_ref[0:1]).reshape(LX, DEPTH, LANES)
     OB[1] = spread(obs_ref[1:2]).reshape(LX, DEPTH, LANES)
 

time: 50.6 us -> 50.6 us (level)
  no operation moved by 1% of the time
where the time goes in v4:
time: 50.6 us; the launch traced here: 50.4 us
  Pallas kernels  46.7 us (92%)
  local copies, waits for them, and re-layouts  2.39 us (5%)
  between operations  1.3 us (3%)
    pallas_call x1, Pallas kernels, run_window(): pl.pallas_call(physics, out_shape=[jax.ShapeDtypeStruct(model.shape, F32)...  46.7 us
    unnamed x4, local copies, waits for them, and re-layouts  2.39 us

profile of v4, /device:TPU:1, one launch (start us, length us, event | category | flops | bytes accessed | tf_op | source)
XLA Modules:
  0.0 50.4 jit_solution(8512581715860252186)
XLA Ops:
  1.3 46.7 %shard_map.113 = (f32[3,32,640]{2,1,0:T(8,128)}, f32[3,32,640]{2,1,0:T(8,128)}) custom-call(f32[3,32,640]{2,1,0:T(8,128)} %bitcast.18, f32[3,32,640]{2,1,0:T(8,128)} %bitcast.19, s32[1,128]{1,0:T(1,128)} %bitcast.24, s32[4,1,32]{2,1,0:T(1,128)} %aper_ref.1, bf16[9,8,32,80]{3,2,1,0:T(8,128)(2,1)} %bitcast.16, bf16[9,8,32,80]{3,2,1,0:T(8,128)(2,1)} %bitcast.17, ...), custom_call_target="tpu_custom_call" | custom-call | tf_op jit(solution)/shard_map/pallas_call | solution.py:591
  48.0 0.0 copy-start
  48.0 1.7 %copy.15 = f32[32,3,640]{2,0,1:T(8,128)} copy(f32[32,3,640]{2,0,1:T(8,128)} %bitcast.21) | data formatting | bytes 491520
  49.7 0.0 copy-done
  49.7 0.7 %copy.16 = f32[32,3,640]{2,0,1:T(8,128)} copy(f32[32,3,640]{2,0,1:T(8,128)S(1)} %bitcast.20) | data formatting | bytes 491520
Async XLA Ops:
  48.0 1.7 %copy-start = (f32[3,32,640]{2,1,0:T(8,128)S(1)}, f32[3,32,640]{2,1,0:T(8,128)}, u32[]{:S(2)}) copy-start(f32[3,32,640]{2,1,0:T(8,128)} %get-tuple-element.5) | copy-start | bytes 737284
